TPU v7x, 32 devices: a whole 2x2x4 slice. The times are simulated.
32 devices in a mesh: section: 2 (over y), dp: 16 (over z, x, core).
Axes of the slice: x: 2, y: 2, z: 4, core: 2. Of those that a mesh axis runs over, the one named last changes fastest.
Arguments:
- tokens: bfloat16 [2, 4096, 576], P(None, 'dp'), may hold values from -6 to 6
- segments: int32 [2, 16, 256], P(None, 'dp'), may hold values from 0 to 3, never falling along the last dimension, each value on 1 to 128 neighbouring positions
- w_query: bfloat16 [2, 331776], P('section', 'dp'), may hold values from -0.375 to 0.375
- w_key: bfloat16 [2, 110592], P('section', 'dp'), may hold values from -0.375 to 0.375
- w_value: bfloat16 [2, 110592], P('section', 'dp'), may hold values from -0.25 to 0.25
- w_out: bfloat16 [2, 331776], P('section', 'dp'), may hold values from -0.75 to 0.75
- w_gate: bfloat16 [2, 884736], P('section', 'dp'), may hold values from -0.25 to 0.25
- w_up: bfloat16 [2, 884736], P('section', 'dp'), may hold values from -0.25 to 0.25
- w_down: bfloat16 [2, 884736], P('section', 'dp'), may hold values from -0.15625 to 0.15625
- attn_gain: float32 [2, 576], P('section'), may hold values from 0.5 to 1.5
- mlp_gain: float32 [2, 576], P('section'), may hold values from 0.5 to 1.5
- out_grad: bfloat16 [2, 4096, 576], P(None, 'dp'), may hold values from -6 to 6
Outputs:
- layer_out: bfloat16 [2, 2, 4096, 576], P('section', None, 'dp')
- input_grad: bfloat16 [2, 2, 4096, 576], P('section', None, 'dp')
- grad_w_query: float32 [2, 331776], P('section', 'dp')
- grad_w_key: float32 [2, 110592], P('section', 'dp')
- grad_w_value: float32 [2, 110592], P('section', 'dp')
- grad_w_out: float32 [2, 331776], P('section', 'dp')
- grad_w_gate: float32 [2, 884736], P('section', 'dp')
- grad_w_up: float32 [2, 884736], P('section', 'dp')
- grad_w_down: float32 [2, 884736], P('section', 'dp')
- grad_attn_gain: float32 [2, 576], P('section')
- grad_mlp_gain: float32 [2, 576], P('section')
Inputs may be any that keep to these rules, and one draw needn't show every extreme that they name: `segments`: segment numbers never fall along a pack of 256 tokens; each document (a run of one number) has 1 to 128 tokens.
All inputs are finite; a program needn't handle non-finite values.
Results may differ from a plain program's by a relative error of at most 0.025.
The roundings to bfloat16 on the way count: a program that leaves them out, or rounds other values in their place, can miss the bound.
Values may be sent and summed in bfloat16 or wider, within the bound.
No kernel may reach another device: no remote copies, remote signals or barrier semaphores. Data moves between devices by JAX's collectives and lax.ppermute only.
A program may use at most 128 MiB of HBM per device.

v0:
```python
import functools
import math

import jax
import jax.numpy as jnp
from jax import lax
from jax.experimental import pallas as pl
from jax.experimental.pallas import tpu as pltpu
from jax.sharding import PartitionSpec as P

D = 576
HEADS = 9
KV_HEADS = 3
HEAD = 64
FF = 1536
TOK_MB = 256
QW = HEADS * HEAD
KVW = KV_HEADS * HEAD
REP = HEADS // KV_HEADS

EPS = 1e-05
THETA = 100000.0
NEG = -1000000000.0

PAD = 640
COL_K = QW
COL_O = QW + KVW
COL_V = COL_O + D
COL_VX = 1280
SKIP_V = COL_V - COL_VX

BF = jnp.bfloat16
F32 = jnp.float32

PARAMS = pltpu.CompilerParams(vmem_limit_bytes=60 * 1024 * 1024)


def dot(left, right):
    return lax.dot_general(left, right, (((1,), (0,)), ((), ())), preferred_element_type=F32)


def dot_nt(left, right):
    return lax.dot_general(left, right, (((1,), (1,)), ((), ())), preferred_element_type=F32)


def dot_tn(left, right):
    return lax.dot_general(left, right, (((0,), (0,)), ((), ())), preferred_element_type=F32)


def spread(rows, place):
    return dot(rows, place).astype(BF)


def collect(rows, place):
    high = rows.astype(BF)
    low = (rows - high.astype(F32)).astype(BF)
    return dot_nt(high, place) + dot_nt(low, place)


def turned(tile):
    lane = lax.broadcasted_iota(jnp.int32, tile.shape, 1)
    return jnp.where(lane % HEAD < HEAD // 2, pltpu.roll(tile, 128 - HEAD // 2, 1), pltpu.roll(tile, HEAD // 2, 1))


def inv_rms(stream):
    return lax.rsqrt(jnp.mean(stream * stream, -1, keepdims=True) + EPS)


def norm_back(stream, gain_row, grad_normed):
    scale_r = inv_rms(stream)
    weighted = grad_normed * gain_row
    grad_stream = scale_r * weighted - stream * scale_r**3 * jnp.mean(
        stream * weighted, -1, keepdims=True
    )
    grad_gain = jnp.sum(grad_normed * stream * scale_r, 0, keepdims=True)
    return (grad_stream, grad_gain)


CHUNK = 768
CHUNKS = FF // CHUNK
HALF = TOK_MB // 2
GROUPS = 16
EACH = PAD // GROUPS
EACH_FF = FF // GROUPS
DV = QW + D + 2 * KVW - COL_VX

ANY = pl.BlockSpec(memory_space=pl.ANY)
SMEM = pl.BlockSpec(memory_space=pltpu.SMEM)
VMEM = pl.BlockSpec(memory_space=pltpu.VMEM)


def shape(*dims, dtype=BF):
    return jax.ShapeDtypeStruct(dims, dtype)


class Names:
    def __getattr__(self, name):
        return name


N = Names()


STORED = dict(
    na=shape(TOK_MB, PAD),
    qk=shape(TOK_MB, COL_O),
    v=shape(TOK_MB, KVW),
    lse=shape(TOK_MB, 128, dtype=F32),
    mx=shape(TOK_MB, PAD),
    mid=shape(TOK_MB, D, dtype=F32),
    nb=shape(TOK_MB, PAD),
    gate=shape(TOK_MB, FF, dtype=F32),
    up=shape(TOK_MB, FF, dtype=F32),
    act=shape(TOK_MB, FF),
)
FOR_BACK = (N.gate, N.up, N.mid, N.qk, N.v, N.lse)
KEPT = dict(
    dqk=shape(TOK_MB, COL_O),
    dv=shape(TOK_MB, DV),
    gattn=shape(TOK_MB, D),
    dg=shape(TOK_MB, FF),
    du=shape(TOK_MB, FF),
)
INPUTS = dict(
    agu=shape(3, PAD, FF),
    c_own=shape(GROUPS // 2, EACH_FF, D),
    c_other=shape(GROUPS // 2, EACH_FF, D),
    down=shape(GROUPS, EACH_FF, D),
    place=shape(D, PAD),
    cos=shape(2, TOK_MB, 128, dtype=F32),
    sin=shape(2, TOK_MB, 128, dtype=F32),
    mask=shape(2, TOK_MB, TOK_MB, dtype=F32),
)
HELD = dict(
    att=shape(PAD, FF),
    gw=shape(PAD, FF),
    uw=shape(PAD, FF),
    down=shape(GROUPS, EACH_FF, D),
    place=shape(D, PAD),
    cos=shape(TOK_MB, 128, dtype=F32),
    sin=shape(TOK_MB, 128, dtype=F32),
    mask=shape(TOK_MB, TOK_MB, dtype=F32),
    x=shape(TOK_MB, D),
    g=shape(TOK_MB, D),
)


class Copies:
    def __init__(self, sems):
        self.sems, self.count, self.open = sems, 0, {}

    def start(self, name, source, target):
        copy = pltpu.make_async_copy(source, target, self.sems.at[self.count])
        self.count += 1
        self.open.setdefault(name, []).append(copy)
        copy.start()

    def start_either(self, name, take_one, one, two, target):
        first = pltpu.make_async_copy(one, target, self.sems.at[self.count])
        second = pltpu.make_async_copy(two, target, self.sems.at[self.count])
        self.count += 1
        self.open.setdefault(name, []).append(first)

        @pl.when(take_one)
        def _():
            first.start()

        @pl.when(jnp.logical_not(take_one))
        def _():
            second.start()

    def wait(self, *names):
        for name in names:
            for copy in self.open.pop(name, ()):
                copy.wait()

    def wait_all(self):
        self.wait(*list(self.open))


def blocks_of_rows():
    return ((0, HALF, HALF), (HALF, TOK_MB, TOK_MB))


def forward(held, kept, copies, ga_ref, gb_ref, note):
    copies.wait(N.x, N.place)
    place = held[N.place][...]
    stream = held[N.x][...].astype(F32)
    normed_a = spread((stream * inv_rms(stream) * ga_ref[...]).astype(BF), place)
    note(N.na, normed_a)
    copies.wait(N.att, N.cos, N.sin)
    raw = dot(normed_a, held[N.att][:, :COL_O])
    cosine, sine = held[N.cos][...], held[N.sin][...]
    tiles = []
    lane = lax.broadcasted_iota(jnp.int32, (TOK_MB, 128), 1)
    for j in range(COL_O // 128):
        tile = raw[:, 128 * j : 128 * (j + 1)]
        tile = (tile * cosine + turned(tile) * sine).astype(BF)
        if 128 * (j + 1) <= QW:
            tile = tile * jnp.asarray(HEAD ** (-0.5), BF)
        elif 128 * j < QW:
            tile = jnp.where(lane < QW - 128 * j, tile.astype(F32) * HEAD ** (-0.5), tile.astype(F32)).astype(BF)
        tiles.append(tile)
    qk = jnp.concatenate(tiles, 1)
    note(N.qk, qk)
    value = dot(normed_a, held[N.att][:, COL_VX:])[:, SKIP_V:].astype(BF)
    note(N.v, value)
    copies.wait(N.mask)
    mixed = []
    for h in range(HEADS):
        kv = h // REP
        key = qk[:, COL_K + HEAD * kv : COL_K + HEAD * (kv + 1)]
        val = value[:, HEAD * kv : HEAD * (kv + 1)]
        parts = []
        for low, high, keys in blocks_of_rows():
            query = qk[low:high, HEAD * h : HEAD * (h + 1)]
            scores = jnp.where(held[N.mask][low:high, :keys] > 0.5, dot_nt(query, key[:keys]), NEG)
            row_max = jnp.max(scores, -1, keepdims=True)
            terms = jnp.exp(scores - row_max)
            total = jnp.sum(terms, -1, keepdims=True)
            attend = (terms * (1.0 / total)).astype(BF)
            parts.append(dot(attend, val[:keys]).astype(BF))
            if kept is not None:
                kept[N.lse][low:high, h : h + 1] = row_max + jnp.log(total)
        mixed.append(jnp.concatenate(parts, 0))
    note(N.lse, None)
    mixed_p = spread(jnp.concatenate(mixed, 1), place)
    note(N.mx, mixed_p)
    middle = stream + dot(mixed_p, held[N.att][:, COL_O : COL_O + D])
    note(N.mid, middle)
    normed_b = spread((middle * inv_rms(middle) * gb_ref[...]).astype(BF), place)
    note(N.nb, normed_b)
    copies.wait(N.gw, N.uw, N.down)
    note(N.laid, None)
    result = middle
    for c in range(0, FF, CHUNK):
        gate = dot(normed_b, held[N.gw][:, c : c + CHUNK])
        up = dot(normed_b, held[N.uw][:, c : c + CHUNK])
        act = (gate * jax.nn.sigmoid(gate) * up).astype(BF)
        result = result + dot(act, down_of(held)[c : c + CHUNK])
        if kept is not None:
            kept[N.gate][:, c : c + CHUNK] = gate
            kept[N.up][:, c : c + CHUNK] = up
            kept[N.act][:, c : c + CHUNK] = act
    note(N.gate, None)
    note(N.up, None)
    note(N.act, None)
    return result.astype(BF)


def down_of(held):
    return held[N.down][...].reshape(FF, D)


def backward(held, kept, copies, ga_ref, gb_ref, note):
    copies.wait(N.g, N.down)
    grad_low = held[N.g][...]
    grad_out = grad_low.astype(F32)
    back_p = jnp.zeros((TOK_MB, PAD), F32)
    down = down_of(held)
    for c in range(0, FF, CHUNK):
        grad_act = dot_nt(grad_low, down[c : c + CHUNK])
        copies.wait(N.gate + str(c), N.up + str(c))
        gate = kept[N.gate][:, c : c + CHUNK]
        up = kept[N.up][:, c : c + CHUNK]
        sig = jax.nn.sigmoid(gate)
        acts = grad_act * sig
        d_gate = (acts * up * (1.0 + gate * (1.0 - sig))).astype(BF)
        d_up = (acts * gate).astype(BF)
        note(N.dg, d_gate, c)
        note(N.du, d_up, c)
        copies.wait(N.gw, N.uw)
        back_p = back_p + dot_nt(d_gate, held[N.gw][:, c : c + CHUNK]) + dot_nt(d_up, held[N.uw][:, c : c + CHUNK])
    copies.wait(N.place, N.mid, N.att)
    place = held[N.place][...]
    back_b, gain_b = norm_back(kept[N.mid][...], gb_ref[...], collect(back_p, place))
    grad_middle = grad_out + back_b
    grad_attn = grad_middle.astype(BF)
    note(N.gattn, grad_attn)
    grad_mixed = dot_nt(dot_nt(grad_attn, held[N.att][:, COL_O : COL_O + D]).astype(BF), place).astype(BF)
    copies.wait(N.qk, N.v, N.lse, N.mask, N.cos, N.sin, N.x)
    d_query, d_key, d_value = [], [], []
    for kv in range(KV_HEADS):
        key = kept[N.qk][:, COL_K + HEAD * kv : COL_K + HEAD * (kv + 1)]
        value = kept[N.v][:, HEAD * kv : HEAD * (kv + 1)]
        sums_k, sums_v = [None, None], [None, None]
        for h in range(kv * REP, (kv + 1) * REP):
            parts = []
            for at, (low, high, keys) in enumerate(blocks_of_rows()):
                query = kept[N.qk][low:high, HEAD * h : HEAD * (h + 1)]
                grad_h = grad_mixed[low:high, HEAD * h : HEAD * (h + 1)]
                scores = jnp.where(held[N.mask][low:high, :keys] > 0.5, dot_nt(query, key[:keys]), NEG)
                attend = jnp.exp(scores - kept[N.lse][low:high, h : h + 1])
                grad_attend = dot_nt(grad_h, value[:keys])
                inner = jnp.sum(attend * grad_attend, -1, keepdims=True)
                grad_scores = (attend * (grad_attend - inner)).astype(BF)
                part_v = dot_tn(attend.astype(BF), grad_h)
                part_k = dot_tn(grad_scores, query)
                sums_v[at] = part_v if sums_v[at] is None else sums_v[at] + part_v
                sums_k[at] = part_k if sums_k[at] is None else sums_k[at] + part_k
                parts.append(dot(grad_scores, key[:keys]) * HEAD ** (-0.5))
            d_query.append(jnp.concatenate(parts, 0))
        d_key.append(jnp.concatenate([sums_k[0] + sums_k[1][:HALF], sums_k[1][HALF:]], 0))
        d_value.append(jnp.concatenate([sums_v[0] + sums_v[1][:HALF], sums_v[1][HALF:]], 0).astype(BF))
    raw = jnp.concatenate(d_query + d_key, 1)
    cosine, sine = held[N.cos][...], held[N.sin][...]
    tiles = []
    for j in range(COL_O // 128):
        tile = raw[:, 128 * j : 128 * (j + 1)]
        tiles.append((tile * cosine - turned(tile) * sine).astype(BF))
    d_qk = jnp.concatenate(tiles, 1)
    d_v = jnp.concatenate([jnp.zeros((TOK_MB, SKIP_V), BF)] + d_value, 1)
    note(N.dqk, d_qk)
    note(N.dv, d_v)
    back_p = dot_nt(d_qk, held[N.att][:, :COL_O]) + dot_nt(d_v, held[N.att][:, COL_VX:])
    back_a, gain_a = norm_back(held[N.x][...].astype(F32), ga_ref[...], collect(back_p, place))
    return (grad_middle + back_a).astype(BF), gain_a, gain_b


SLOTS = dict(
    lead=(N.forward,),
    both=(N.forward, N.backward, N.store),
    ahead=(N.forward, N.store),
    behind=(N.backward, N.keep),
)


def layer_kernel(name, micro, names, refs):
    does = SLOTS[name]
    ref = dict(zip(names, refs))
    held = {key: ref["held_" + key] for key in HELD if "held_" + key in ref}
    kept = {key: ref["kept_" + key] for key in STORED if "kept_" + key in ref} or None
    section = ref[N.coords][3]
    index = {N.zero: 0, N.one: 1, N.same: section, N.other: 1 - section}[micro]
    copies = Copies(ref[N.sems])

    def bring(key):
        copies.start(key, ref[key].at[index], held[key])

    def bring_x():
        if N.arrived in ref:
            copies.start_either(N.x, section == 0, ref[N.tokens].at[index], ref[N.arrived], held[N.x])
        else:
            copies.start(N.x, ref[N.tokens].at[index], held[N.x])

    def bring_weights(order):
        for key in order:
            if key == N.down:
                if N.down in ref:
                    copies.start(key, ref[N.down], held[N.down])
                    continue
                own_z, own_x, own_c = (ref[N.coords][i] for i in range(3))
                for at in range(GROUPS // 2):
                    chip = lax.bitwise_xor(own_z, at // 2) * 2 + lax.bitwise_xor(own_x, at % 2)
                    copies.start(key, ref[N.c_own].at[at], held[N.down].at[chip * 2 + own_c])
                    copies.start(key, ref[N.c_other].at[at], held[N.down].at[chip * 2 + 1 - own_c])
            elif key == N.place:
                copies.start(key, ref[N.place], held[N.place])
            else:
                copies.start(key, ref[N.agu].at[(N.att, N.gw, N.uw).index(key)], held[key])

    def bring_g():
        if N.arrived_grad in ref:
            copies.start_either(N.g, section == 0, ref[N.arrived_grad], ref[N.out_grad].at[index], held[N.g])
        else:
            copies.start(N.g, ref[N.out_grad].at[index], held[N.g])

    if N.forward in does:
        bring_x()
        bring_weights([N.place, N.att])
        bring(N.cos)
        bring(N.sin)
        bring(N.mask)
        bring_weights([N.gw, N.uw, N.down])
        if N.backward in does:
            bring_g()
    else:
        bring_g()
        bring_weights([N.down])
        for c in range(0, FF, CHUNK):
            for key in (N.gate, N.up):
                copies.start(key + str(c), ref["stored_" + key].at[:, c : c + CHUNK], kept[key].at[:, c : c + CHUNK])
        bring_weights([N.gw, N.uw, N.place])
        copies.start(N.mid, ref[N.stored_mid], kept[N.mid])
        bring_weights([N.att])
        for key in (N.qk, N.v, N.lse):
            copies.start(key, ref["stored_" + key], kept[key])
        bring(N.mask)
        bring(N.cos)
        bring(N.sin)
        bring_x()

    def note_stored(key, value, column=None):
        if key == N.laid:
            if N.laid in ref:
                copies.start(N.laid, held[N.down], ref[N.laid])
            return
        if N.store in does:
            if value is not None:
                kept[key][...] = value
            copies.start("out_" + key, kept[key], ref["store_" + key])

    def note_kept(key, value, column=None):
        if N.keep in does:
            if column is None:
                ref["made_" + key][...] = value
            else:
                ref["made_" + key][:, column : column + CHUNK] = value
            if column in (None, FF - CHUNK):
                copies.start("out_" + key, ref["made_" + key], ref["keep_" + key])

    if N.forward in does:
        ref[N.out][...] = forward(held, kept, copies, ref[N.ga], ref[N.gb], note_stored)
    if N.backward in does:
        grad, gain_a, gain_b = backward(held, kept, copies, ref[N.ga], ref[N.gb], note_kept)
        ref[N.in_grad][...] = grad
        if N.keep in does:
            ref[N.gains][0:1, :] = gain_a
            ref[N.gains][1:2, :] = gain_b
    copies.wait_all()


def run_layer(name, micro, common, tokens, arrived=None, out_grad=None, arrived_grad=None, stored=None):
    does = SLOTS[name]
    operands = dict(coords=common[N.coords], tokens=tokens, ga=common[N.ga], gb=common[N.gb])
    operands.update({key: common[key] for key in INPUTS if key in common})
    specs = dict(coords=SMEM, ga=VMEM, gb=VMEM)
    if arrived is not None:
        operands[N.arrived] = arrived
    if N.backward in does:
        operands[N.out_grad] = out_grad
        if arrived_grad is not None:
            operands[N.arrived_grad] = arrived_grad
    if stored is not None:
        operands.update({"stored_" + key: stored[key] for key in FOR_BACK})
    outs, out_specs = {}, []
    if N.forward in does:
        outs[N.out] = shape(TOK_MB, D)
    if N.down not in common:
        outs[N.laid] = INPUTS[N.down]
    if N.backward in does:
        outs[N.in_grad] = shape(TOK_MB, D)
    if N.keep in does:
        outs[N.gains] = shape(2, D, dtype=F32)
        outs.update({"keep_" + key: KEPT[key] for key in KEPT})
    if N.store in does:
        outs.update({"store_" + key: STORED[key] for key in STORED})
    out_specs = [ANY if key.startswith(("store_", "keep_", "laid")) else VMEM for key in outs]
    scratch = {"held_" + key: pltpu.VMEM(h.shape, h.dtype) for key, h in HELD.items() if key != N.g or N.backward in does}
    if name != N.lead:
        hold = STORED if N.forward in does else FOR_BACK
        scratch.update({"kept_" + key: pltpu.VMEM(STORED[key].shape, STORED[key].dtype) for key in hold})
    if N.keep in does:
        scratch.update({"made_" + key: pltpu.VMEM(KEPT[key].shape, BF) for key in KEPT})
    scratch[N.sems] = pltpu.SemaphoreType.DMA((28 if N.down in common else 44,))
    names = list(operands) + list(outs) + list(scratch)

    def kernel(*refs):
        layer_kernel(name, micro, names, refs)

    results = pl.pallas_call(
        kernel,
        out_shape=list(outs.values()),
        in_specs=[specs.get(key, ANY) for key in operands],
        out_specs=out_specs,
        scratch_shapes=list(scratch.values()),
        compiler_params=PARAMS,
        name="layer_" + name,
    )(*operands.values())
    return dict(zip(outs, results))


PAIRS = (N.act, N.g, N.nb, N.dg, N.du, N.mx, N.gattn, N.na, N.dqk, N.dv)


def slab_of(block):
    return jnp.concatenate(
        [
            jnp.concatenate([block[8 * i : 8 * i + 8, 128 * j : 128 * j + 128] for i in range(EACH_FF // 8)], 1)
            for j in range(PAD // 128)
        ],
        0,
    )


def block_of(slab):
    tiles = slab.reshape(slab.shape[:-2] + (PAD // 128, 8, EACH_FF // 8, 128))
    return jnp.moveaxis(tiles, -2, -4).swapaxes(-3, -2).reshape(slab.shape[:-2] + (EACH_FF, PAD))


def weights_kernel(names, refs):
    ref = dict(zip(names, refs))
    copies = Copies(ref[N.sems])
    own_z, own_x, own_c, section = (ref[N.coords][i] for i in range(4))
    for key in PAIRS:
        for at in range(2):
            target = ref["in_" + key].at[pl.ds(TOK_MB * at, TOK_MB)]
            if key == N.g:
                copies.start_either(
                    key, section == 0, ref["grad_%d" % at], ref[N.out_grad].at[section if at == 0 else 1 - section], target
                )
            else:
                copies.start(key, ref["%s_%d" % (key, at)], target)

    def put_pairs(keep_ref, send_ref, at, columns, blocks, pair):
        for one, two in zip(blocks[::2], blocks[1::2]):
            far, across = lax.bitwise_xor(own_z, pair // 2), lax.bitwise_xor(own_x, pair % 2)
            index = (across, far) + at + (slice(None), columns)
            keep_ref[index] = jnp.where(own_c == 0, one, two).astype(BF)
            send_ref[index] = jnp.where(own_c == 0, two, one).astype(BF)
            pair += 1

    def put(keep_ref, send_ref, at, columns, rows):
        put_pairs(keep_ref, send_ref, at, columns, jnp.split(rows, GROUPS), 0)

    copies.wait(N.act, N.g)
    grad_down = jnp.concatenate([ref[N.in_g][...], jnp.zeros((2 * TOK_MB, PAD - D), BF)], 1)
    step = 4 * EACH_FF
    for c in range(0, FF, step):
        slabs = [slab_of(piece) for piece in jnp.split(dot_tn(ref[N.in_act][:, c : c + step], grad_down), 4)]
        put_pairs(ref[N.keep_m], ref[N.send_m], (3,), slice(0, FF), slabs, c // step * 2)
    copies.wait(N.nb, N.dg, N.du)
    normed_b = ref[N.in_nb][...]
    for at, key in ((1, N.dg), (2, N.du)):
        for c in range(0, FF, CHUNK):
            put(ref[N.keep_m], ref[N.send_m], (at,), slice(c, c + CHUNK), dot_tn(normed_b, ref["in_" + key][:, c : c + CHUNK]))
    copies.wait(N.mx, N.gattn, N.na, N.dqk, N.dv)
    normed_a, mixed = ref[N.in_na][...], ref[N.in_mx][...]
    put(ref[N.keep_m], ref[N.send_m], (0,), slice(0, COL_O), dot_tn(normed_a, ref[N.in_dqk][...]))
    put(ref[N.keep_m], ref[N.send_m], (0,), slice(COL_O, COL_VX), dot_tn(mixed, ref[N.in_gattn][:, : COL_VX - COL_O]))
    grad_o = dot_tn(mixed, ref[N.in_gattn][:, COL_VX - COL_O :])
    grad_o = jnp.concatenate([grad_o, jnp.zeros((PAD, KVW), F32)], 1)
    put(ref[N.keep_m], ref[N.send_m], (0,), slice(COL_VX, FF), dot_tn(normed_a, ref[N.in_dv][...]) + grad_o)
    copies.start(N.out, ref[N.send_m], ref[N.out_send_m])
    copies.start(N.out, ref[N.keep_m], ref[N.out_keep_m])
    copies.wait_all()


def run_weights(coords, rows, grads, out_grad):
    operands = dict(coords=coords, out_grad=out_grad)
    for at in range(2):
        operands["grad_%d" % at] = grads[at]
        operands.update({"%s_%d" % (key, at): rows[at][key] for key in PAIRS if key != N.g})
    main = shape(2, 4, 4, EACH, FF)
    outs = dict(out_keep_m=main, out_send_m=main)
    columns = {key: (STORED | KEPT | {N.g: HELD[N.g]})[key].shape[1] for key in PAIRS}
    scratch = {"in_" + key: pltpu.VMEM((2 * TOK_MB, columns[key]), BF) for key in PAIRS}
    scratch.update({key[4:]: pltpu.VMEM(out.shape, BF) for key, out in outs.items()})
    scratch[N.sems] = pltpu.SemaphoreType.DMA((24,))
    names = list(operands) + list(outs) + list(scratch)

    def kernel(*refs):
        weights_kernel(names, refs)

    results = pl.pallas_call(
        kernel,
        out_shape=list(outs.values()),
        in_specs=[SMEM] + [ANY] * (len(operands) - 1),
        out_specs=[ANY] * len(outs),
        scratch_shapes=list(scratch.values()),
        compiler_params=PARAMS,
        name=N.weight_grads,
    )(*operands.values())
    return dict(zip(outs, results))


def make_tables(seg_row):
    count_t = seg_row.shape[0]
    order_idx = jnp.arange(count_t, dtype=jnp.int32)
    same_doc = seg_row[:, None] == seg_row[None, :]
    before = order_idx[None, :] < order_idx[:, None]
    positions = jnp.sum(jnp.where(same_doc & before, jnp.float32(1.0), jnp.float32(0.0)), axis=1)
    allowed = same_doc & (order_idx[None, :] <= order_idx[:, None])
    inv_freq = jnp.exp(jnp.arange(HEAD // 2, dtype=jnp.float32) * (-2.0 * math.log(THETA) / HEAD))
    angles = positions[:, None] * inv_freq[None, :]
    cosine, sine = jnp.cos(angles), jnp.sin(angles)
    cosine = jnp.concatenate([cosine] * 4, -1)
    sine = jnp.concatenate([-sine, sine] * 2, -1)
    return (cosine, sine, allowed.astype(F32))


def placement(rows_each, rows_padded):
    row = lax.broadcasted_iota(jnp.int32, (D, PAD), 0)
    col = lax.broadcasted_iota(jnp.int32, (D, PAD), 1)
    return (col == row + (row // rows_each) * (rows_padded - rows_each)).astype(BF)


def place_of(z, x, c):
    return (z * 2 + x) * 2 + c


PLACES = [(z, x, c) for z in range(4) for x in range(2) for c in range(2)]


def moved(value, dz, dx, dc):
    return lax.ppermute(value, "dp", [(place_of(z, x, c), place_of(z ^ dz, x ^ dx, c ^ dc)) for z, x, c in PLACES])


def gather_weights(shard, owners):
    w_query, w_key, w_value, w_out, w_gate, w_up, w_down = shard
    if owners == GROUPS:
        rows = D // owners
        att = jnp.concatenate(
            [w_query.reshape(rows, QW), w_key.reshape(rows, KVW), w_out.reshape(rows, D), w_value.reshape(rows, KVW)], 1
        )
        packed = jnp.stack([att, w_gate.reshape(rows, FF), w_up.reshape(rows, FF)])
        packed = jnp.pad(packed, ((0, 0), (0, EACH - rows), (0, 0)))
        agu = lax.all_gather(packed, "dp", axis=1, tiled=True)
        w_down = w_down.reshape(EACH_FF, D)
        lines = [w_down] + [moved(w_down, dz, 0, 0) for dz in (1, 2, 3)]
        c_own = jnp.stack([block for line in lines for block in (line, moved(line, 0, 1, 0))])
        c_other = moved(c_own, 0, 0, 1)
        c_own, c_other, corner = lax.optimization_barrier((c_own, c_other, w_down[:8, :128]))
        met = lax.all_gather(corner, "dp", axis=0, tiled=False)
        corner = lax.dynamic_index_in_dim(met, lax.axis_index("dp"), 0, keepdims=False)
        c_own = c_own.at[0, :8, :128].set(corner)
        return agu, c_own, c_other, placement(rows, EACH)
    w_query, w_key, w_value, w_out, w_gate, w_up, w_down = (
        lax.all_gather(member[0], "dp", axis=0, tiled=True) for member in shard
    )
    att = jnp.concatenate(
        [w_query.reshape(D, QW), w_key.reshape(D, KVW), w_out.reshape(QW, D), w_value.reshape(D, KVW)], 1
    )
    agu = jnp.pad(jnp.stack([att, w_gate.reshape(D, FF), w_up.reshape(D, FF)]), ((0, 0), (0, PAD - D), (0, 0)))
    down = w_down.reshape(GROUPS // 2, 2, EACH_FF, D)
    return agu, down[:, 0], down[:, 1], placement(D, D)


def cut(att):
    return att[:, :QW], att[:, COL_K:COL_O], att[:, COL_V:], att[:, COL_O:COL_V]


def add(*terms):
    return sum(term.astype(F32) for term in terms)


def sum_of_four(value, others):
    return (value + others[0]) + (others[1] + others[2])


def reduce_blocks(keep, send, gains):
    near = [moved(gains, 0, 0, 1), moved(gains, 0, 1, 0), moved(gains, 0, 1, 1)]
    got = moved(send, 0, 0, 1)
    got, near = lax.optimization_barrier((got, near))
    gains = sum_of_four(gains, near)
    wide = [moved(gains, 1, 0, 0), moved(gains, 2, 0, 0), moved(gains, 3, 0, 0)]
    blocks = [add(keep[1, far], got[1, far]).astype(BF) for far in range(4)]
    across_three, across_two = moved(blocks[3], 0, 1, 0), moved(blocks[2], 0, 1, 0)
    across_three, wide = lax.optimization_barrier((across_three, wide))
    gains = sum_of_four(gains, wide)
    three = add(keep[0, 3], got[0, 3], across_three).astype(BF)
    three, last_one = lax.optimization_barrier((three, blocks[1]))
    beside_three, across_one = moved(three, 1, 0, 0), moved(last_one, 0, 1, 0)
    across_two, last_zero = lax.optimization_barrier((across_two, blocks[0]))
    across_zero = moved(last_zero, 0, 1, 0)
    far_two = moved(add(keep[0, 2], got[0, 2], across_two, beside_three).astype(BF), 2, 0, 0)
    beside_one = moved(add(keep[0, 1], got[0, 1], across_one).astype(BF), 1, 0, 0)
    return add(keep[0, 0], got[0, 0], across_zero, far_two, beside_one), gains


def scatter_grads(out, gains, owners):
    if owners == GROUPS:
        main, gains = reduce_blocks(out[N.out_keep_m], out[N.out_send_m], gains)
        rows = D // owners
        att, gate, up = main[0, :rows], main[1, :rows], main[2, :rows]
        down = block_of(main[3])[:, :D]
        return tuple(piece.reshape(1, -1) for piece in cut(att) + (gate, up, down)) + (gains[0:1], gains[1:2])
    main = jnp.stack([out[N.out_keep_m], out[N.out_send_m]]).transpose(3, 2, 1, 0, 4, 5).reshape(4, GROUPS, EACH, FF)
    down = block_of(main[3])[:, :, :D].reshape(FF, D)
    main = main[:3].reshape(3, PAD, FF)[:, :D]
    pieces = cut(main[0]) + (main[1], main[2], down)
    gains = lax.psum(gains, "dp")
    return tuple(
        lax.psum_scatter(piece.reshape(owners, -1), "dp", scatter_dimension=0, tiled=True).astype(F32) for piece in pieces
    ) + (gains[0:1], gains[1:2])


def shards(
    tokens,
    segments,
    w_query,
    w_key,
    w_value,
    w_out,
    w_gate,
    w_up,
    w_down,
    attn_gain,
    mlp_gain,
    out_grad,
):
    section = lax.axis_index("section")
    first = section == 0
    owners = lax.axis_size("dp")
    me = lax.axis_index("dp") if owners == GROUPS else 0
    coords = jnp.stack([me // 4, me // 2 % 2, me % 2, section, 0, 0, 0, 0]).astype(jnp.int32)
    agu, c_own, c_other, place = gather_weights((w_query, w_key, w_value, w_out, w_gate, w_up, w_down), owners)
    cosine, sine, mask = jax.vmap(make_tables)(segments[:, 0])
    agu, c_own, c_other, place, cosine, sine, mask, tokens, out_grad, coords = lax.optimization_barrier(
        (agu, c_own, c_other, place, cosine, sine, mask, tokens, out_grad, coords)
    )
    common = dict(
        agu=agu, c_own=c_own, c_other=c_other, place=place, cos=cosine, sin=sine, mask=mask, coords=coords, ga=attn_gain, gb=mlp_gain
    )

    def send_on(block):
        return lax.ppermute(block, "section", [(0, 1)])

    def send_back(block):
        return lax.ppermute(block, "section", [(1, 0)])

    def stored_of(outs):
        return {key: outs["store_" + key] for key in STORED}

    def rows_of(stored, outs):
        return stored | {key: outs["keep_" + key] for key in KEPT}

    first_out = run_layer(N.lead, N.zero, common, tokens)
    lead_zero = first_out[N.out]
    common = {key: common[key] for key in common if key not in (N.c_own, N.c_other)} | {N.down: first_out[N.laid]}
    arrived_zero = send_on(lead_zero)
    lead_one = run_layer(N.lead, N.one, common, tokens)[N.out]
    arrived_one = send_on(lead_one)
    two = run_layer(N.both, N.other, common, tokens, arrived_zero, out_grad)
    arrived_grad = send_back(two[N.in_grad])
    four = run_layer(N.ahead, N.same, common, tokens, arrived_one)
    stored_two, stored_four = stored_of(two), stored_of(four)
    five = run_layer(N.behind, N.same, common, tokens, arrived_one, out_grad, arrived_grad, stored_four)
    last_grad = send_back(five[N.in_grad])
    six = run_layer(N.behind, N.other, common, tokens, arrived_zero, out_grad, last_grad, stored_two)
    grads = run_weights(
        coords, (rows_of(stored_four, five), rows_of(stored_two, six)), (arrived_grad, last_grad), out_grad
    )
    shares = scatter_grads(grads, five[N.gains] + six[N.gains], owners)
    layer_out = jnp.stack([jnp.where(first, four[N.out], two[N.out]), jnp.where(first, two[N.out], four[N.out])])
    input_grad = jnp.stack([jnp.where(first, five[N.in_grad], six[N.in_grad]), jnp.where(first, six[N.in_grad], five[N.in_grad])])
    return (layer_out[None], input_grad[None], *shares)


def solution(mesh):
    weights = (P("section", "dp"),) * 7
    gains = (P("section", None),) * 2
    rows = P("section", None, "dp", None)
    return jax.shard_map(
        shards,
        mesh=mesh,
        in_specs=(P(None, "dp", None), P(None, "dp", None), *weights, *gains, P(None, "dp", None)),
        out_specs=(rows, rows, *weights, *gains),
        check_vma=False,
    )
```

profile of v0, /device:TPU:0, one launch (start us, length us, event | category | flops | bytes accessed | tf_op | source)
XLA Modules:
  0.0 293.3 jit_solution(11927475710420324236)
XLA Ops:
  16.7 5.1 %collective-permute-start.5 = (bf16[96,576]{1,0:T(8,128)(2,1)S(1)}, bf16[96,576]{1,0:T(8,128)(2,1)S(1)}, u32[]{:S(2)}, u32[]{:S(2)}) collective-permute-start(bf16[96,576]{1,0:T(8,128)(2,1)S(1)} %reshape.154), channel_id=1, source_target_pairs={{0,12},{1,13},{2,14},{3,15},{4,8},{5,9},{6,10},{7,11},{8,4},{9,5},... | collective-permute-start | bytes 331784 | tf_op jit(solution)/shard_map/ppermute | solution.py:596
  27.8 9.5 %collective-permute-done.3 = bf16[96,576]{1,0:T(8,128)(2,1)S(1)} collective-permute-done((bf16[96,576]{1,0:T(8,128)(2,1)S(1)}, bf16[96,576]{1,0:T(8,128)(2,1)S(1)}, u32[]{:S(2)}, u32[]{:S(2)}) %collective-permute-start.3) | collective-permute-done | bytes 110624 | tf_op jit(solution)/shard_map/ppermute | solution.py:596
  39.4 4.5 %collective-permute-done.2 = bf16[96,576]{1,0:T(8,128)(2,1)S(1)} collective-permute-done((bf16[96,576]{1,0:T(8,128)(2,1)S(1)}, bf16[96,576]{1,0:T(8,128)(2,1)S(1)}, u32[]{:S(2)}, u32[]{:S(2)}) %collective-permute-start.2) | collective-permute-done | bytes 110624 | tf_op jit(solution)/shard_map/ppermute | solution.py:596
  49.3 23.1 %all-gather = bf16[128,128]{1,0:T(8,128)(2,1)S(1)} all-gather(bf16[8,128]{1,0:T(8,128)(2,1)S(1)} %slice.138), channel_id=2, replica_groups=mesh['section'=2,'dp'=16] {'dp'}, dimensions={0}, use_global_device_ids=true | all-gather | bytes 34816 | tf_op jit(solution)/shard_map/all_gather | solution.py:614
  72.4 8.5 %all-gather.3.cloned.1.call-done.refs_4_ = bf16[3,640,1536]{2,1,0:T(8,128)(2,1)} async-done(((bf16[3,40,1536]{2,1,0:T(8,128)(2,1)}), bf16[3,640,1536]{2,1,0:T(8,128)(2,1)}) %all-gather.3.cloned.1.call-update) | async-done | bytes 5898256 | tf_op jit(solution)/shard_map/all_gather | solution.py:608
  82.1 11.0 %layer_lead.2 = (bf16[256,576]{1,0:T(8,128)(2,1)}, bf16[16,96,576]{2,1,0:T(8,128)(2,1)}) custom-call(s32[8]{0:T(128)} %stack.77.refs_0_, bf16[2,256,576]{2,1,0:T(8,128)(2,1)} %copy.37.refs_1_, f32[1,576]{1,0:T(1,128)} %refs_2_.11, f32[1,576]{1,0:T(1,128)} %refs_3_.11, bf16[3,640,1536]{2,1,0:T(8,128)(2,1)} %all-gather.3.cloned.1.call-done.refs_4_, ...), custom_call_target="tpu_custom_call" | custom-call | tf_op jit(solution)/shard_map/layer_lead/pallas_call | solution.py:461
  93.0 3.4 %collective-permute-start.9 = (bf16[256,576]{1,0:T(8,128)(2,1)}, bf16[256,576]{1,0:T(8,128)(2,1)S(1)}, u32[]{:S(2)}, u32[]{:S(2)}) collective-permute-start(bf16[256,576]{1,0:T(8,128)(2,1)} %get-tuple-element.103), channel_id=1, source_target_pairs={{0,16},{1,17},{2,18},{3,19},{4,20},{5,21},{6,22},{7,23},{8,24},{9,... | collective-permute-start | bytes 884744 | tf_op jit(solution)/shard_map/ppermute | solution.py:707
  96.5 10.9 %layer_lead.3 = bf16[256,576]{1,0:T(8,128)(2,1)} custom-call(s32[8]{0:T(128)} %stack.77.refs_0_, bf16[2,256,576]{2,1,0:T(8,128)(2,1)} %copy.37.refs_1_, f32[1,576]{1,0:T(1,128)} %refs_2_.11, f32[1,576]{1,0:T(1,128)} %refs_3_.11, bf16[3,640,1536]{2,1,0:T(8,128)(2,1)} %all-gather.3.cloned.1.call-done.refs_4_, bf16[16,96,576]{2,1,0:T(8,128)(2,1)} %get-tuple-element.101.refs_5_, ...), custom_call_target="tpu_custom_call" | custom-call | tf_op jit(solution)/shard_map/layer_lead/pallas_call | solution.py:461
  111.0 22.6 %layer_both.1 = (bf16[256,576]{1,0:T(8,128)(2,1)}, bf16[256,576]{1,0:T(8,128)(2,1)}, bf16[256,640]{1,0:T(8,128)(2,1)}, bf16[256,768]{1,0:T(8,128)(2,1)}, bf16[25...) custom-call(s32[8]{0:T(128)} %stack.77.refs_0_, ...), custom_call_target="tpu_custom_call" | custom-call | tf_op jit(solution)/shard_map/layer_both/pallas_call | solution.py:461
  135.6 12.2 %layer_ahead.1 = (bf16[256,576]{1,0:T(8,128)(2,1)}, bf16[256,640]{1,0:T(8,128)(2,1)}, bf16[256,768]{1,0:T(8,128)(2,1)}, bf16[256,192]{1,0:T(8,128)(2,1)}, f32[25...) custom-call(s32[8]{0:T(128)} %stack.77.refs_0_, ...), custom_call_target="tpu_custom_call" | custom-call | tf_op jit(solution)/shard_map/layer_ahead/pallas_call | solution.py:461
  148.6 17.4 %layer_behind.2 = (bf16[256,576]{1,0:T(8,128)(2,1)}, f32[2,576]{1,0:T(2,128)}, bf16[256,768]{1,0:T(8,128)(2,1)}, bf16[256,256]{1,0:T(8,128)(2,1)}, bf16[256,576]...) custom-call(s32[8]{0:T(128)} %stack.77.refs_0_, bf16[2,256,576]{2,1,0:T(8,128)(2,1)} %copy.37.refs_1_, ...), custom_call_target="tpu_custom_call" | custom-call | tf_op jit(solution)/shard_map/layer_behind/pallas_call | solution.py:461
  167.3 10.4 %collective-permute-done.11.refs_12_ = bf16[256,576]{1,0:T(8,128)(2,1)S(1)} collective-permute-done((bf16[256,576]{1,0:T(8,128)(2,1)}, bf16[256,576]{1,0:T(8,128)(2,1)S(1)}, u32[]{:S(2)}, u32[]{:S(2)}) %collective-permute-start.11) | collective-permute-done | bytes 294944 | tf_op jit(solution)/shard_map/ppermute | solution.py:710
  178.5 17.2 %layer_behind.3 = (bf16[256,576]{1,0:T(8,128)(2,1)}, f32[2,576]{1,0:T(2,128)}, bf16[256,768]{1,0:T(8,128)(2,1)}, bf16[256,256]{1,0:T(8,128)(2,1)}, bf16[256,576]...) custom-call(s32[8]{0:T(128)} %stack.77.refs_0_, bf16[2,256,576]{2,1,0:T(8,128)(2,1)} %copy.37.refs_1_, ...), custom_call_target="tpu_custom_call" | custom-call | tf_op jit(solution)/shard_map/layer_behind/pallas_call | solution.py:461
  195.8 10.8 %weight_grads.1 = (bf16[2,4,4,40,1536]{4,3,2,1,0:T(8,128)(2,1)}, bf16[2,4,4,40,1536]{4,3,2,1,0:T(8,128)(2,1)}) custom-call(s32[8]{0:T(128)} %stack.77.refs_0_, bf16[2,256,576]{2,1,0:T(8,128)(2,1)} %copy.39.refs_11_.refs_1_, bf16[256,576]{1,0:T(8,128)(2,1)} %copy-done.2, bf16[256,1536]{1,0:T(8,128)(2,1)} %get-tuple-element.121.refs_3_, ...), custom_call_target="tpu_custom_call" | custom-call | tf_op jit(solution)/shard_map/weight_grads/pallas_call | solution.py:555
  211.0 2.4 collective-permute-done.13
  213.6 3.4 %fusion.12 = (bf16[4,40,1536]{2,1,0:T(8,128)(2,1)S(1)}, bf16[4,40,1536]{2,1,0:T(8,128)(2,1)S(1)}, bf16[4,40,1536]{2,1,0:T(8,128)(2,1)S(1)}, bf16[4,40,1536]{2,1,0:T(8,128)(2,1)S(1)}) fusion(bf16[2,4,4,40,1536]{4,3,2,1,0:T(8,128)(2,1)S(1)} %collective-permute-done.12, bf16[2,4,4,40,1536]{4,3,2,1,0:T(8,128)(2,1)} %get-tuple-element.139), kind=kLoop, calls=%fused_computation.27 | loop fusion | flops 3932160 | bytes 5898240 | tf_op jit(solution)/shard_map/convert_element_type | solution.py:647
  224.3 6.9 %collective-permute-done.18 = bf16[4,40,1536]{2,1,0:T(8,128)(2,1)S(1)} collective-permute-done((bf16[4,40,1536]{2,1,0:T(8,128)(2,1)S(1)}, bf16[4,40,1536]{2,1,0:T(8,128)(2,1)S(1)}, u32[]{:S(2)}, u32[]{:S(2)}) %collective-permute-start.18) | collective-permute-done | bytes 491552 | tf_op jit(solution)/shard_map/ppermute | solution.py:596
  231.2 2.1 fusion.2
  238.7 3.0 %collective-permute-done.16 = bf16[4,40,1536]{2,1,0:T(8,128)(2,1)S(1)} collective-permute-done((bf16[4,40,1536]{2,1,0:T(8,128)(2,1)S(1)}, bf16[4,40,1536]{2,1,0:T(8,128)(2,1)S(1)}, u32[]{:S(2)}, u32[]{:S(2)}) %collective-permute-start.16) | collective-permute-done | bytes 491552 | tf_op jit(solution)/shard_map/ppermute | solution.py:596
  242.3 2.9 collective-permute-done.22
  245.2 7.2 %collective-permute-done.24 = bf16[4,40,1536]{2,1,0:T(8,128)(2,1)} collective-permute-done((bf16[4,40,1536]{2,1,0:T(8,128)(2,1)S(1)}, bf16[4,40,1536]{2,1,0:T(8,128)(2,1)}, u32[]{:S(2)}, u32[]{:S(2)}) %collective-permute-start.24) | collective-permute-done | bytes 491552 | tf_op jit(solution)/shard_map/ppermute | solution.py:596
  252.4 3.0 %fusion.4 = (bf16[4,40,1536]{2,1,0:T(8,128)(2,1)}, bf16[4,40,1536]{2,1,0:T(8,128)(2,1)}) fusion(bf16[4,40,1536]{2,1,0:T(8,128)(2,1)S(1)} %collective-permute-done.22, bf16[4,40,1536]{2,1,0:T(8,128)(2,1)S(1)} %collective-permute-done.16, bf16[2,4,4,40,1536]{4,3,2,1,0:T(8,128)(2,1)} %copy-done, bf16[2,4,4,40,1536]{4,3,2,1,0:T(8,128)(2,1)} %get-tuple-element.139, ...), kind=kLoop, calls=%fused_computation.8 | loop fusion | flops 3440640 | bytes 4423680 | tf_op jit(solution)/shard_map/convert_element_type | solution.py:656
  259.7 2.3 collective-permute-done.17
  262.0 16.7 %collective-permute-done.23 = bf16[4,40,1536]{2,1,0:T(8,128)(2,1)S(1)} collective-permute-done((bf16[4,40,1536]{2,1,0:T(8,128)(2,1)}, bf16[4,40,1536]{2,1,0:T(8,128)(2,1)S(1)}, u32[]{:S(2)}, u32[]{:S(2)}) %collective-permute-start.23) | collective-permute-done | bytes 491552 | tf_op jit(solution)/shard_map/ppermute | solution.py:596
  (134 shorter events, 61.4 us)
Async XLA Ops:
  7.2 73.8 %all-gather.3.cloned.1.call-start = ((), (), s32[]{:S(2)}) async-start(), calls=%async_computation | async-start | bytes 6266880 | tf_op jit(solution)/shard_map/all_gather | solution.py:608
  16.7 9.4 %collective-permute-start.5 = (bf16[96,576]{1,0:T(8,128)(2,1)S(1)}, bf16[96,576]{1,0:T(8,128)(2,1)S(1)}, u32[]{:S(2)}, u32[]{:S(2)}) collective-permute-start(bf16[96,576]{1,0:T(8,128)(2,1)S(1)} %reshape.154), channel_id=1, source_target_pairs={{0,12},{1,13},{2,14},{3,15},{4,8},{5,9},{6,10},{7,11},{8,4},{9,5},... | collective-permute-start | bytes 331784 | tf_op jit(solution)/shard_map/ppermute | solution.py:596
  21.8 15.5 %collective-permute-start.3 = (bf16[96,576]{1,0:T(8,128)(2,1)S(1)}, bf16[96,576]{1,0:T(8,128)(2,1)S(1)}, u32[]{:S(2)}, u32[]{:S(2)}) collective-permute-start(bf16[96,576]{1,0:T(8,128)(2,1)S(1)} %reshape.154), channel_id=1, source_target_pairs={{0,8},{1,9},{2,10},{3,11},{4,12},{5,13},{6,14},{7,15},{8,0},{9,1},... | collective-permute-start | bytes 331784 | tf_op jit(solution)/shard_map/ppermute | solution.py:596
  21.8 17.2 %collective-permute-start.1 = (bf16[96,576]{1,0:T(8,128)(2,1)S(1)}, bf16[96,576]{1,0:T(8,128)(2,1)S(1)}, u32[]{:S(2)}, u32[]{:S(2)}) collective-permute-start(bf16[96,576]{1,0:T(8,128)(2,1)S(1)} %reshape.154), channel_id=1, source_target_pairs={{0,4},{1,5},{2,6},{3,7},{4,0},{5,1},{6,2},{7,3},{8,12},{9,13},{10,... | collective-permute-start | bytes 331784 | tf_op jit(solution)/shard_map/ppermute | solution.py:596
  22.5 16.9 %collective-permute-start = (bf16[96,576]{1,0:T(8,128)(2,1)S(1)}, bf16[96,576]{1,0:T(8,128)(2,1)S(1)}, u32[]{:S(2)}, u32[]{:S(2)}) collective-permute-start(bf16[96,576]{1,0:T(8,128)(2,1)S(1)} %reshape.154), channel_id=1, source_target_pairs={{0,2},{1,3},{2,0},{3,1},{4,6},{5,7},{6,4},{7,5},{8,10},{9,11},{10,... | collective-permute-start | bytes 331784 | tf_op jit(solution)/shard_map/ppermute | solution.py:596
  26.1 18.0 %collective-permute-start.6 = (bf16[96,576]{1,0:T(8,128)(2,1)S(1)}, bf16[96,576]{1,0:T(8,128)(2,1)S(1)}, u32[]{:S(2)}, u32[]{:S(2)}) collective-permute-start(bf16[96,576]{1,0:T(8,128)(2,1)S(1)} %collective-permute-done.5), channel_id=1, source_target_pairs={{0,2},{1,3},{2,0},{3,1},{4,6},{5,7},{6,4},{7,5},{8,10},{9,11},{10,... | collective-permute-start | bytes 331784 | tf_op jit(solution)/shard_map/ppermute | solution.py:596
  37.3 6.7 %collective-permute-start.4 = (bf16[96,576]{1,0:T(8,128)(2,1)S(1)}, bf16[96,576]{1,0:T(8,128)(2,1)S(1)}, u32[]{:S(2)}, u32[]{:S(2)}) collective-permute-start(bf16[96,576]{1,0:T(8,128)(2,1)S(1)} %collective-permute-done.3), channel_id=1, source_target_pairs={{0,2},{1,3},{2,0},{3,1},{4,6},{5,7},{6,4},{7,5},{8,10},{9,11},{10,... | collective-permute-start | bytes 331784 | tf_op jit(solution)/shard_map/ppermute | solution.py:596
  39.1 4.9 %collective-permute-start.2 = (bf16[96,576]{1,0:T(8,128)(2,1)S(1)}, bf16[96,576]{1,0:T(8,128)(2,1)S(1)}, u32[]{:S(2)}, u32[]{:S(2)}) collective-permute-start(bf16[96,576]{1,0:T(8,128)(2,1)S(1)} %collective-permute-done.1), channel_id=1, source_target_pairs={{0,2},{1,3},{2,0},{3,1},{4,6},{5,7},{6,4},{7,5},{8,10},{9,11},{10,... | collective-permute-start | bytes 331784 | tf_op jit(solution)/shard_map/ppermute | solution.py:596
  44.1 5.2 %collective-permute-start.7 = (bf16[8,96,576]{2,1,0:T(8,128)(2,1)S(1)}, bf16[8,96,576]{2,1,0:T(8,128)(2,1)S(1)}, u32[]{:S(2)}, u32[]{:S(2)}) collective-permute-start(bf16[8,96,576]{2,1,0:T(8,128)(2,1)S(1)} %bitcast_dynamic-update-slice_fusion), channel_id=1, source_target_pairs={{0,1},{1,0},{2,3},{3,2},{4,5},{5,4},{6,7},{7,6},{8,9},{9,8},{10,11... | collective-permute-start | bytes 2654216 | tf_op jit(solution)/shard_map/ppermute | solution.py:596
  93.0 17.2 %collective-permute-start.9 = (bf16[256,576]{1,0:T(8,128)(2,1)}, bf16[256,576]{1,0:T(8,128)(2,1)S(1)}, u32[]{:S(2)}, u32[]{:S(2)}) collective-permute-start(bf16[256,576]{1,0:T(8,128)(2,1)} %get-tuple-element.103), channel_id=1, source_target_pairs={{0,16},{1,17},{2,18},{3,19},{4,20},{5,21},{6,22},{7,23},{8,24},{9,... | collective-permute-start | bytes 884744 | tf_op jit(solution)/shard_map/ppermute | solution.py:707
  107.4 27.5 %collective-permute-start.8 = (bf16[256,576]{1,0:T(8,128)(2,1)}, bf16[256,576]{1,0:T(8,128)(2,1)S(1)}, u32[]{:S(2)}, u32[]{:S(2)}) collective-permute-start(bf16[256,576]{1,0:T(8,128)(2,1)} %layer_lead.3), channel_id=1, source_target_pairs={{0,16},{1,17},{2,18},{3,19},{4,20},{5,21},{6,22},{7,23},{8,24},{9,... | collective-permute-start | bytes 884744 | tf_op jit(solution)/shard_map/ppermute | solution.py:707
  133.6 14.3 %collective-permute-start.10 = (bf16[256,576]{1,0:T(8,128)(2,1)}, bf16[256,576]{1,0:T(8,128)(2,1)S(1)}, u32[]{:S(2)}, u32[]{:S(2)}) collective-permute-start(bf16[256,576]{1,0:T(8,128)(2,1)} %get-tuple-element.106), channel_id=1, source_target_pairs={{16,0},{17,1},{18,2},{19,3},{20,4},{21,5},{22,6},{23,7},{24,8},{25... | collective-permute-start | bytes 884744 | tf_op jit(solution)/shard_map/ppermute | solution.py:710
  166.0 11.7 %collective-permute-start.11 = (bf16[256,576]{1,0:T(8,128)(2,1)}, bf16[256,576]{1,0:T(8,128)(2,1)S(1)}, u32[]{:S(2)}, u32[]{:S(2)}) collective-permute-start(bf16[256,576]{1,0:T(8,128)(2,1)} %get-tuple-element.113), channel_id=1, source_target_pairs={{16,0},{17,1},{18,2},{19,3},{20,4},{21,5},{22,6},{23,7},{24,8},{25... | collective-permute-start | bytes 884744 | tf_op jit(solution)/shard_map/ppermute | solution.py:710
  206.6 7.1 %collective-permute-start.12 = (bf16[2,4,4,40,1536]{4,3,2,1,0:T(8,128)(2,1)}, bf16[2,4,4,40,1536]{4,3,2,1,0:T(8,128)(2,1)S(1)}, u32[]{:S(2)}, u32[]{:S(2)}) collective-permute-start(bf16[2,4,4,40,1536]{4,3,2,1,0:T(8,128)(2,1)} %get-tuple-element.140), channel_id=1, source_target_pairs={{0,1},{1,0},{2,3},{3,2},{4,5},{5,4},{6,7},{7,6},{8,9},{9,8},{10,11... | collective-permute-start | bytes 11796488 | tf_op jit(solution)/shard_map/ppermute | solution.py:596
  208.9 4.6 %collective-permute-start.13 = (f32[2,576]{1,0:T(2,128)S(1)}, f32[2,576]{1,0:T(2,128)S(1)}, u32[]{:S(2)}, u32[]{:S(2)}) collective-permute-start(f32[2,576]{1,0:T(2,128)S(1)} %add.108), channel_id=1, source_target_pairs={{0,1},{1,0},{2,3},{3,2},{4,5},{5,4},{6,7},{7,6},{8,9},{9,8},{10,11... | collective-permute-start | bytes 13832 | tf_op jit(solution)/shard_map/ppermute | solution.py:596
  217.1 14.1 %collective-permute-start.18 = (bf16[4,40,1536]{2,1,0:T(8,128)(2,1)S(1)}, bf16[4,40,1536]{2,1,0:T(8,128)(2,1)S(1)}, u32[]{:S(2)}, u32[]{:S(2)}) collective-permute-start(bf16[4,40,1536]{2,1,0:T(8,128)(2,1)S(1)} %get-tuple-element.181), channel_id=1, source_target_pairs={{0,2},{1,3},{2,0},{3,1},{4,6},{5,7},{6,4},{7,5},{8,10},{9,11},{10,... | collective-permute-start | bytes 1474568 | tf_op jit(solution)/shard_map/ppermute | solution.py:596
  217.7 5.9 %collective-permute-start.21 = (f32[2,576]{1,0:T(2,128)S(1)}, f32[2,576]{1,0:T(2,128)S(1)}, u32[]{:S(2)}, u32[]{:S(2)}) collective-permute-start(f32[2,576]{1,0:T(2,128)S(1)} %add_add_fusion.1), channel_id=1, source_target_pairs={{0,12},{1,13},{2,14},{3,15},{4,8},{5,9},{6,10},{7,11},{8,4},{9,5},... | collective-permute-start | bytes 13832 | tf_op jit(solution)/shard_map/ppermute | solution.py:596
  219.7 4.5 %collective-permute-start.20 = (f32[2,576]{1,0:T(2,128)S(1)}, f32[2,576]{1,0:T(2,128)S(1)}, u32[]{:S(2)}, u32[]{:S(2)}) collective-permute-start(f32[2,576]{1,0:T(2,128)S(1)} %add_add_fusion.1), channel_id=1, source_target_pairs={{0,8},{1,9},{2,10},{3,11},{4,12},{5,13},{6,14},{7,15},{8,0},{9,1},... | collective-permute-start | bytes 13832 | tf_op jit(solution)/shard_map/ppermute | solution.py:596
  222.1 19.6 %collective-permute-start.16 = (bf16[4,40,1536]{2,1,0:T(8,128)(2,1)S(1)}, bf16[4,40,1536]{2,1,0:T(8,128)(2,1)S(1)}, u32[]{:S(2)}, u32[]{:S(2)}) collective-permute-start(bf16[4,40,1536]{2,1,0:T(8,128)(2,1)S(1)} %get-tuple-element.182), channel_id=1, source_target_pairs={{0,2},{1,3},{2,0},{3,1},{4,6},{5,7},{6,4},{7,5},{8,10},{9,11},{10,... | collective-permute-start | bytes 1474568 | tf_op jit(solution)/shard_map/ppermute | solution.py:596
  233.3 11.8 %collective-permute-start.22 = (bf16[4,40,1536]{2,1,0:T(8,128)(2,1)}, bf16[4,40,1536]{2,1,0:T(8,128)(2,1)S(1)}, u32[]{:S(2)}, u32[]{:S(2)}) collective-permute-start(bf16[4,40,1536]{2,1,0:T(8,128)(2,1)} %fusion.2), channel_id=1, source_target_pairs={{0,4},{1,5},{2,6},{3,7},{4,0},{5,1},{6,2},{7,3},{8,12},{9,13},{10,... | collective-permute-start | bytes 1474568 | tf_op jit(solution)/shard_map/ppermute | solution.py:596
  234.8 17.6 %collective-permute-start.24 = (bf16[4,40,1536]{2,1,0:T(8,128)(2,1)S(1)}, bf16[4,40,1536]{2,1,0:T(8,128)(2,1)}, u32[]{:S(2)}, u32[]{:S(2)}) collective-permute-start(bf16[4,40,1536]{2,1,0:T(8,128)(2,1)S(1)} %get-tuple-element.151), channel_id=1, source_target_pairs={{0,2},{1,3},{2,0},{3,1},{4,6},{5,7},{6,4},{7,5},{8,10},{9,11},{10,... | collective-permute-start | bytes 1474568 | tf_op jit(solution)/shard_map/ppermute | solution.py:596
  241.7 20.3 %collective-permute-start.17 = (bf16[4,40,1536]{2,1,0:T(8,128)(2,1)S(1)}, bf16[4,40,1536]{2,1,0:T(8,128)(2,1)S(1)}, u32[]{:S(2)}, u32[]{:S(2)}) collective-permute-start(bf16[4,40,1536]{2,1,0:T(8,128)(2,1)S(1)} %get-tuple-element.144), channel_id=1, source_target_pairs={{0,2},{1,3},{2,0},{3,1},{4,6},{5,7},{6,4},{7,5},{8,10},{9,11},{10,... | collective-permute-start | bytes 1474568 | tf_op jit(solution)/shard_map/ppermute | solution.py:596
  255.4 23.3 %collective-permute-start.23 = (bf16[4,40,1536]{2,1,0:T(8,128)(2,1)}, bf16[4,40,1536]{2,1,0:T(8,128)(2,1)S(1)}, u32[]{:S(2)}, u32[]{:S(2)}) collective-permute-start(bf16[4,40,1536]{2,1,0:T(8,128)(2,1)} %get-tuple-element.177), channel_id=1, source_target_pairs={{0,8},{1,9},{2,10},{3,11},{4,12},{5,13},{6,14},{7,15},{8,0},{9,1},... | collective-permute-start | bytes 1474568 | tf_op jit(solution)/shard_map/ppermute | solution.py:596
  257.3 21.4 %collective-permute-start.25 = (bf16[4,40,1536]{2,1,0:T(8,128)(2,1)}, bf16[4,40,1536]{2,1,0:T(8,128)(2,1)S(1)}, u32[]{:S(2)}, u32[]{:S(2)}) collective-permute-start(bf16[4,40,1536]{2,1,0:T(8,128)(2,1)} %get-tuple-element.178), channel_id=1, source_target_pairs={{0,4},{1,5},{2,6},{3,7},{4,0},{5,1},{6,2},{7,3},{8,12},{9,13},{10,... | collective-permute-start | bytes 1474568 | tf_op jit(solution)/shard_map/ppermute | solution.py:596
  (17 other events, 174.7 us)
Sparse Core Ops, SparseCore 0:
  16.0 64.8 all-gather.2
where the time goes:
time: 299 us; the launch traced here: 293 us
  Pallas kernels  102 us (34%)
  waiting for transfers between devices  79 us (26%)
  starting transfers between devices  32.8 us (11%)
  other arithmetic  25.7 us (9%)
  blocking collectives  23.1 us (8%)
  local copies, waits for them, and re-layouts  15.5 us (5%)
  between operations  15 us (5%)
    pallas_call x6, Pallas kernels, run_layer(): pl.pallas_call(kernel, out_shape=list(outs.values()), in_specs=[specs.get...  91.3 us
    ppermute x22, waiting for transfers between devices, moved(): lax.ppermute(value, 'dp', [(place_of(z, x, c), place_of(z ^ dz, x ^ dx, c...  60 us
    ppermute x22, starting transfers between devices, moved(): lax.ppermute(value, 'dp', [(place_of(z, x, c), place_of(z ^ dz, x ^ dx, c...  25 us
    all_gather x1, blocking collectives, gather_weights(): met = lax.all_gather(corner, 'dp', axis=0, tiled=False)  23.1 us
    pallas_call x1, Pallas kernels, run_weights(): pl.pallas_call(kernel, out_shape=list(outs.values()), in_specs=[SMEM] + [...  10.8 us
    ppermute x2, waiting for transfers between devices, send_back(): return lax.ppermute(block, 'section', [(1, 0)])  10.4 us
    all_gather x1, waiting for transfers between devices, gather_weights(): agu = lax.all_gather(packed, 'dp', axis=1, tiled=True)  8.52 us
    unnamed x7, other arithmetic  7.69 us
  transfers between devices with their start and end apart: 27, of which 17 were waited for; matrix products, arithmetic and copies ran while one was open for 6% of the time, Pallas kernels for 16%

commit v1 on v0

--- a/solution.py
+++ b/solution.py
@@ -322,6 +322,7 @@
     both=(N.forward, N.backward, N.store),
     ahead=(N.forward, N.store),
     behind=(N.backward, N.keep),
+    last=(N.backward, N.weights),
 )
 
 
@@ -400,7 +401,25 @@
                 kept[key][...] = value
             copies.start("out_" + key, kept[key], ref["store_" + key])
 
+    if N.weights in does:
+        for key in PAIRS:
+            half = ref["in_" + key].at[pl.ds(0, TOK_MB)]
+            if key == N.g:
+                copies.start_either(key + "_0", section == 0, ref[N.grad_0], ref[N.out_grad].at[section], half)
+            else:
+                copies.start(key, ref[key + "_0"], half)
+        for key in (N.act, N.nb, N.mx, N.na):
+            copies.start(key, ref[key + "_1"], ref["in_" + key].at[pl.ds(TOK_MB, TOK_MB)])
+        feed_forward, attention = weight_parts(ref, copies)
+
     def note_kept(key, value, column=None):
+        if N.weights in does:
+            columns = slice(None) if column is None else slice(column, column + CHUNK)
+            ref["in_" + key][TOK_MB:, columns] = value
+            if key == N.gattn:
+                copies.wait(N.g + "_0")
+                ref[N.in_g][TOK_MB:, :] = held[N.g][...]
+                feed_forward()
         if N.keep in does:
             if column is None:
                 ref["made_" + key][...] = value
@@ -414,13 +433,15 @@
     if N.backward in does:
         grad, gain_a, gain_b = backward(held, kept, copies, ref[N.ga], ref[N.gb], note_kept)
         ref[N.in_grad][...] = grad
-        if N.keep in does:
+        if N.weights in does:
+            attention()
+        if N.keep in does or N.weights in does:
             ref[N.gains][0:1, :] = gain_a
             ref[N.gains][1:2, :] = gain_b
     copies.wait_all()
 
 
-def run_layer(name, micro, common, tokens, arrived=None, out_grad=None, arrived_grad=None, stored=None):
+def run_layer(name, micro, common, tokens, arrived=None, out_grad=None, arrived_grad=None, stored=None, rows=None, first_grad=None):
     does = SLOTS[name]
     operands = dict(coords=common[N.coords], tokens=tokens, ga=common[N.ga], gb=common[N.gb])
     operands.update({key: common[key] for key in INPUTS if key in common})
@@ -433,6 +454,10 @@
             operands[N.arrived_grad] = arrived_grad
     if stored is not None:
         operands.update({"stored_" + key: stored[key] for key in FOR_BACK})
+    if N.weights in does:
+        operands.update({key + "_0": rows[key] for key in PAIRS if key != N.g})
+        operands.update({key + "_1": stored[key] for key in (N.act, N.nb, N.mx, N.na)})
+        operands[N.grad_0] = first_grad
     outs, out_specs = {}, []
     if N.forward in does:
         outs[N.out] = shape(TOK_MB, D)
@@ -440,19 +465,26 @@
         outs[N.laid] = INPUTS[N.down]
     if N.backward in does:
         outs[N.in_grad] = shape(TOK_MB, D)
+    if N.weights in does:
+        outs[N.gains] = shape(2, D, dtype=F32)
+        outs.update({key: shape(2, 4, 4, EACH, FF) for key in (N.out_keep_m, N.out_send_m)})
     if N.keep in does:
         outs[N.gains] = shape(2, D, dtype=F32)
         outs.update({"keep_" + key: KEPT[key] for key in KEPT})
     if N.store in does:
         outs.update({"store_" + key: STORED[key] for key in STORED})
-    out_specs = [ANY if key.startswith(("store_", "keep_", "laid")) else VMEM for key in outs]
+    out_specs = [ANY if key.startswith(("store_", "keep_", "laid", "out_")) else VMEM for key in outs]
     scratch = {"held_" + key: pltpu.VMEM(h.shape, h.dtype) for key, h in HELD.items() if key != N.g or N.backward in does}
     if name != N.lead:
         hold = STORED if N.forward in does else FOR_BACK
         scratch.update({"kept_" + key: pltpu.VMEM(STORED[key].shape, STORED[key].dtype) for key in hold})
     if N.keep in does:
         scratch.update({"made_" + key: pltpu.VMEM(KEPT[key].shape, BF) for key in KEPT})
-    scratch[N.sems] = pltpu.SemaphoreType.DMA((28 if N.down in common else 44,))
+    if N.weights in does:
+        columns = {key: (STORED | KEPT | {N.g: HELD[N.g]})[key].shape[1] for key in PAIRS}
+        scratch.update({"in_" + key: pltpu.VMEM((2 * TOK_MB, columns[key]), BF) for key in PAIRS})
+        scratch.update({key: pltpu.VMEM((2, 4, 4, EACH, FF), BF) for key in (N.keep_m, N.send_m)})
+    scratch[N.sems] = pltpu.SemaphoreType.DMA((48 if N.weights in does else 28 if N.down in common else 44,))
     names = list(operands) + list(outs) + list(scratch)
 
     def kernel(*refs):
@@ -488,19 +520,8 @@
     return jnp.moveaxis(tiles, -2, -4).swapaxes(-3, -2).reshape(slab.shape[:-2] + (EACH_FF, PAD))
 
 
-def weights_kernel(names, refs):
-    ref = dict(zip(names, refs))
-    copies = Copies(ref[N.sems])
-    own_z, own_x, own_c, section = (ref[N.coords][i] for i in range(4))
-    for key in PAIRS:
-        for at in range(2):
-            target = ref["in_" + key].at[pl.ds(TOK_MB * at, TOK_MB)]
-            if key == N.g:
-                copies.start_either(
-                    key, section == 0, ref["grad_%d" % at], ref[N.out_grad].at[section if at == 0 else 1 - section], target
-                )
-            else:
-                copies.start(key, ref["%s_%d" % (key, at)], target)
+def weight_parts(ref, copies):
+    own_z, own_x, own_c = (ref[N.coords][i] for i in range(3))
 
     def put_pairs(keep_ref, send_ref, at, columns, blocks, pair):
         for one, two in zip(blocks[::2], blocks[1::2]):
@@ -513,55 +534,34 @@
     def put(keep_ref, send_ref, at, columns, rows):
         put_pairs(keep_ref, send_ref, at, columns, jnp.split(rows, GROUPS), 0)
 
-    copies.wait(N.act, N.g)
-    grad_down = jnp.concatenate([ref[N.in_g][...], jnp.zeros((2 * TOK_MB, PAD - D), BF)], 1)
-    step = 4 * EACH_FF
-    for c in range(0, FF, step):
-        slabs = [slab_of(piece) for piece in jnp.split(dot_tn(ref[N.in_act][:, c : c + step], grad_down), 4)]
-        put_pairs(ref[N.keep_m], ref[N.send_m], (3,), slice(0, FF), slabs, c // step * 2)
-    copies.wait(N.nb, N.dg, N.du)
-    normed_b = ref[N.in_nb][...]
-    for at, key in ((1, N.dg), (2, N.du)):
-        for c in range(0, FF, CHUNK):
-            put(ref[N.keep_m], ref[N.send_m], (at,), slice(c, c + CHUNK), dot_tn(normed_b, ref["in_" + key][:, c : c + CHUNK]))
-    copies.wait(N.mx, N.gattn, N.na, N.dqk, N.dv)
-    normed_a, mixed = ref[N.in_na][...], ref[N.in_mx][...]
-    put(ref[N.keep_m], ref[N.send_m], (0,), slice(0, COL_O), dot_tn(normed_a, ref[N.in_dqk][...]))
-    put(ref[N.keep_m], ref[N.send_m], (0,), slice(COL_O, COL_VX), dot_tn(mixed, ref[N.in_gattn][:, : COL_VX - COL_O]))
-    grad_o = dot_tn(mixed, ref[N.in_gattn][:, COL_VX - COL_O :])
-    grad_o = jnp.concatenate([grad_o, jnp.zeros((PAD, KVW), F32)], 1)
-    put(ref[N.keep_m], ref[N.send_m], (0,), slice(COL_VX, FF), dot_tn(normed_a, ref[N.in_dv][...]) + grad_o)
-    copies.start(N.out, ref[N.send_m], ref[N.out_send_m])
-    copies.start(N.out, ref[N.keep_m], ref[N.out_keep_m])
-    copies.wait_all()
-
-
-def run_weights(coords, rows, grads, out_grad):
-    operands = dict(coords=coords, out_grad=out_grad)
-    for at in range(2):
-        operands["grad_%d" % at] = grads[at]
-        operands.update({"%s_%d" % (key, at): rows[at][key] for key in PAIRS if key != N.g})
-    main = shape(2, 4, 4, EACH, FF)
-    outs = dict(out_keep_m=main, out_send_m=main)
-    columns = {key: (STORED | KEPT | {N.g: HELD[N.g]})[key].shape[1] for key in PAIRS}
-    scratch = {"in_" + key: pltpu.VMEM((2 * TOK_MB, columns[key]), BF) for key in PAIRS}
-    scratch.update({key[4:]: pltpu.VMEM(out.shape, BF) for key, out in outs.items()})
-    scratch[N.sems] = pltpu.SemaphoreType.DMA((24,))
-    names = list(operands) + list(outs) + list(scratch)
-
-    def kernel(*refs):
-        weights_kernel(names, refs)
-
-    results = pl.pallas_call(
-        kernel,
-        out_shape=list(outs.values()),
-        in_specs=[SMEM] + [ANY] * (len(operands) - 1),
-        out_specs=[ANY] * len(outs),
-        scratch_shapes=list(scratch.values()),
-        compiler_params=PARAMS,
-        name=N.weight_grads,
-    )(*operands.values())
-    return dict(zip(outs, results))
+    def feed_forward():
+        copies.wait(N.act, N.g)
+        grad_down = jnp.concatenate([ref[N.in_g][...], jnp.zeros((2 * TOK_MB, PAD - D), BF)], 1)
+        step = 4 * EACH_FF
+        for c in range(0, FF, step):
+            slabs = [slab_of(piece) for piece in jnp.split(dot_tn(ref[N.in_act][:, c : c + step], grad_down), 4)]
+            put_pairs(ref[N.keep_m], ref[N.send_m], (3,), slice(0, FF), slabs, c // step * 2)
+        copies.wait(N.nb, N.dg, N.du)
+        normed_b = ref[N.in_nb][...]
+        for at, key in ((1, N.dg), (2, N.du)):
+            for c in range(0, FF, CHUNK):
+                put(ref[N.keep_m], ref[N.send_m], (at,), slice(c, c + CHUNK), dot_tn(normed_b, ref["in_" + key][:, c : c + CHUNK]))
+        for slab in range(1, 4):
+            copies.start(N.out, ref[N.send_m].at[:, :, slab], ref[N.out_send_m].at[:, :, slab])
+            copies.start(N.out, ref[N.keep_m].at[:, :, slab], ref[N.out_keep_m].at[:, :, slab])
+
+    def attention():
+        copies.wait(N.mx, N.gattn, N.na, N.dqk, N.dv)
+        normed_a, mixed = ref[N.in_na][...], ref[N.in_mx][...]
+        put(ref[N.keep_m], ref[N.send_m], (0,), slice(0, COL_O), dot_tn(normed_a, ref[N.in_dqk][...]))
+        put(ref[N.keep_m], ref[N.send_m], (0,), slice(COL_O, COL_VX), dot_tn(mixed, ref[N.in_gattn][:, : COL_VX - COL_O]))
+        grad_o = dot_tn(mixed, ref[N.in_gattn][:, COL_VX - COL_O :])
+        grad_o = jnp.concatenate([grad_o, jnp.zeros((PAD, KVW), F32)], 1)
+        put(ref[N.keep_m], ref[N.send_m], (0,), slice(COL_VX, FF), dot_tn(normed_a, ref[N.in_dv][...]) + grad_o)
+        copies.start(N.out, ref[N.send_m].at[:, :, 0], ref[N.out_send_m].at[:, :, 0])
+        copies.start(N.out, ref[N.keep_m].at[:, :, 0], ref[N.out_keep_m].at[:, :, 0])
+
+    return feed_forward, attention
 
 
 def make_tables(seg_row):
@@ -727,10 +727,10 @@
     stored_two, stored_four = stored_of(two), stored_of(four)
     five = run_layer(N.behind, N.same, common, tokens, arrived_one, out_grad, arrived_grad, stored_four)
     last_grad = send_back(five[N.in_grad])
-    six = run_layer(N.behind, N.other, common, tokens, arrived_zero, out_grad, last_grad, stored_two)
-    grads = run_weights(
-        coords, (rows_of(stored_four, five), rows_of(stored_two, six)), (arrived_grad, last_grad), out_grad
+    six = run_layer(
+        N.last, N.other, common, tokens, arrived_zero, out_grad, last_grad, stored_two, rows_of(stored_four, five), arrived_grad
     )
+    grads = six
     shares = scatter_grads(grads, five[N.gains] + six[N.gains], owners)
     layer_out = jnp.stack([jnp.where(first, four[N.out], two[N.out]), jnp.where(first, two[N.out], four[N.out])])
     input_grad = jnp.stack([jnp.where(first, five[N.in_grad], six[N.in_grad]), jnp.where(first, six[N.in_grad], five[N.in_grad])])

time: 299 us -> 295 us (0.987)
  Pallas kernels: 102 us -> 98.2 us
    pallas_call x1 -> x0, Pallas kernels: 10.8 us -> none  [run_weights(): pl.pallas_call(kernel, out_shape=list(outs.values()), in_specs=[SMEM] + [...]
    pallas_call x6, Pallas kernels: 91.3 us -> 98.2 us  [run_layer(): pl.pallas_call(kernel, out_shape=list(outs.values()), in_specs=[specs.get...]
    unnamed x41 -> x39, local copies, waits for them, and re-layouts: 7.12 us -> 7.09 us
where the time goes in v1:
time: 295 us; the launch traced here: 289 us
  Pallas kernels  98.2 us (33%)
  waiting for transfers between devices  78.3 us (27%)
  starting transfers between devices  32.8 us (11%)
  other arithmetic  26.3 us (9%)
  blocking collectives  23.2 us (8%)
  local copies, waits for them, and re-layouts  15.5 us (5%)
  between operations  15 us (5%)
    pallas_call x6, Pallas kernels, run_layer(): pl.pallas_call(kernel, out_shape=list(outs.values()), in_specs=[specs.get...  98.2 us
    ppermute x22, waiting for transfers between devices, moved(): lax.ppermute(value, 'dp', [(place_of(z, x, c), place_of(z ^ dz, x ^ dx, c...  59.4 us
    ppermute x22, starting transfers between devices, moved(): lax.ppermute(value, 'dp', [(place_of(z, x, c), place_of(z ^ dz, x ^ dx, c...  25 us
    all_gather x1, blocking collectives, gather_weights(): met = lax.all_gather(corner, 'dp', axis=0, tiled=False)  23.2 us
    ppermute x2, waiting for transfers between devices, send_back(): return lax.ppermute(block, 'section', [(1, 0)])  10.4 us
    all_gather x1, waiting for transfers between devices, gather_weights(): agu = lax.all_gather(packed, 'dp', axis=1, tiled=True)  8.44 us
    unnamed x7, other arithmetic  7.69 us
    unnamed x39, local copies, waits for them, and re-layouts  7.09 us
  transfers between devices with their start and end apart: 27, of which 17 were waited for; matrix products, arithmetic and copies ran while one was open for 6% of the time, Pallas kernels for 16%

profile of v1, /device:TPU:0, one launch (start us, length us, event | category | flops | bytes accessed | tf_op | source)
XLA Modules:
  0.0 289.4 jit_solution(15144908949064019107)
XLA Ops:
  16.7 5.1 %collective-permute-start.5 = (bf16[96,576]{1,0:T(8,128)(2,1)S(1)}, bf16[96,576]{1,0:T(8,128)(2,1)S(1)}, u32[]{:S(2)}, u32[]{:S(2)}) collective-permute-start(bf16[96,576]{1,0:T(8,128)(2,1)S(1)} %reshape.154), channel_id=1, source_target_pairs={{0,12},{1,13},{2,14},{3,15},{4,8},{5,9},{6,10},{7,11},{8,4},{9,5},... | collective-permute-start | bytes 331784 | tf_op jit(solution)/shard_map/ppermute | solution.py:596
  27.8 9.5 %collective-permute-done.3 = bf16[96,576]{1,0:T(8,128)(2,1)S(1)} collective-permute-done((bf16[96,576]{1,0:T(8,128)(2,1)S(1)}, bf16[96,576]{1,0:T(8,128)(2,1)S(1)}, u32[]{:S(2)}, u32[]{:S(2)}) %collective-permute-start.3) | collective-permute-done | bytes 110624 | tf_op jit(solution)/shard_map/ppermute | solution.py:596
  39.4 4.5 %collective-permute-done.2 = bf16[96,576]{1,0:T(8,128)(2,1)S(1)} collective-permute-done((bf16[96,576]{1,0:T(8,128)(2,1)S(1)}, bf16[96,576]{1,0:T(8,128)(2,1)S(1)}, u32[]{:S(2)}, u32[]{:S(2)}) %collective-permute-start.2) | collective-permute-done | bytes 110624 | tf_op jit(solution)/shard_map/ppermute | solution.py:596
  49.3 23.2 %all-gather = bf16[128,128]{1,0:T(8,128)(2,1)S(1)} all-gather(bf16[8,128]{1,0:T(8,128)(2,1)S(1)} %slice.138), channel_id=2, replica_groups=mesh['section'=2,'dp'=16] {'dp'}, dimensions={0}, use_global_device_ids=true | all-gather | bytes 34816 | tf_op jit(solution)/shard_map/all_gather | solution.py:614
  72.5 8.4 %all-gather.3.cloned.1.call-done.refs_4_ = bf16[3,640,1536]{2,1,0:T(8,128)(2,1)} async-done(((bf16[3,40,1536]{2,1,0:T(8,128)(2,1)}), bf16[3,640,1536]{2,1,0:T(8,128)(2,1)}) %all-gather.3.cloned.1.call-update) | async-done | bytes 5898256 | tf_op jit(solution)/shard_map/all_gather | solution.py:608
  82.1 11.0 %layer_lead.2 = (bf16[256,576]{1,0:T(8,128)(2,1)}, bf16[16,96,576]{2,1,0:T(8,128)(2,1)}) custom-call(s32[8]{0:T(128)} %stack.77.refs_0_, bf16[2,256,576]{2,1,0:T(8,128)(2,1)} %copy.36.refs_1_, f32[1,576]{1,0:T(1,128)} %refs_2_.11, f32[1,576]{1,0:T(1,128)} %refs_3_.11, bf16[3,640,1536]{2,1,0:T(8,128)(2,1)} %all-gather.3.cloned.1.call-done.refs_4_, ...), custom_call_target="tpu_custom_call" | custom-call | tf_op jit(solution)/shard_map/layer_lead/pallas_call | solution.py:493
  93.0 3.4 %collective-permute-start.9 = (bf16[256,576]{1,0:T(8,128)(2,1)}, bf16[256,576]{1,0:T(8,128)(2,1)S(1)}, u32[]{:S(2)}, u32[]{:S(2)}) collective-permute-start(bf16[256,576]{1,0:T(8,128)(2,1)} %get-tuple-element.98), channel_id=1, source_target_pairs={{0,16},{1,17},{2,18},{3,19},{4,20},{5,21},{6,22},{7,23},{8,24},{9,... | collective-permute-start | bytes 884744 | tf_op jit(solution)/shard_map/ppermute | solution.py:707
  96.5 10.9 %layer_lead.3 = bf16[256,576]{1,0:T(8,128)(2,1)} custom-call(s32[8]{0:T(128)} %stack.77.refs_0_, bf16[2,256,576]{2,1,0:T(8,128)(2,1)} %copy.36.refs_1_, f32[1,576]{1,0:T(1,128)} %refs_2_.11, f32[1,576]{1,0:T(1,128)} %refs_3_.11, bf16[3,640,1536]{2,1,0:T(8,128)(2,1)} %all-gather.3.cloned.1.call-done.refs_4_, bf16[16,96,576]{2,1,0:T(8,128)(2,1)} %get-tuple-element.96.refs_5_, ...), custom_call_target="tpu_custom_call" | custom-call | tf_op jit(solution)/shard_map/layer_lead/pallas_call | solution.py:493
  111.0 22.6 %layer_both.1 = (bf16[256,576]{1,0:T(8,128)(2,1)}, bf16[256,576]{1,0:T(8,128)(2,1)}, bf16[256,640]{1,0:T(8,128)(2,1)}, bf16[256,768]{1,0:T(8,128)(2,1)}, bf16[25...) custom-call(s32[8]{0:T(128)} %stack.77.refs_0_, ...), custom_call_target="tpu_custom_call" | custom-call | tf_op jit(solution)/shard_map/layer_both/pallas_call | solution.py:493
  135.6 12.3 %layer_ahead.1 = (bf16[256,576]{1,0:T(8,128)(2,1)}, bf16[256,640]{1,0:T(8,128)(2,1)}, bf16[256,768]{1,0:T(8,128)(2,1)}, bf16[256,192]{1,0:T(8,128)(2,1)}, f32[25...) custom-call(s32[8]{0:T(128)} %stack.77.refs_0_, ...), custom_call_target="tpu_custom_call" | custom-call | tf_op jit(solution)/shard_map/layer_ahead/pallas_call | solution.py:493
  148.7 17.4 %layer_behind.1 = (bf16[256,576]{1,0:T(8,128)(2,1)}, f32[2,576]{1,0:T(2,128)}, bf16[256,768]{1,0:T(8,128)(2,1)}, bf16[256,256]{1,0:T(8,128)(2,1)}, bf16[256,576]...) custom-call(s32[8]{0:T(128)} %stack.77.refs_0_, bf16[2,256,576]{2,1,0:T(8,128)(2,1)} %copy.36.refs_1_, ...), custom_call_target="tpu_custom_call" | custom-call | tf_op jit(solution)/shard_map/layer_behind/pallas_call | solution.py:493
  167.4 10.4 %collective-permute-done.11.refs_12_ = bf16[256,576]{1,0:T(8,128)(2,1)S(1)} collective-permute-done((bf16[256,576]{1,0:T(8,128)(2,1)}, bf16[256,576]{1,0:T(8,128)(2,1)S(1)}, u32[]{:S(2)}, u32[]{:S(2)}) %collective-permute-start.11) | collective-permute-done | bytes 294944 | tf_op jit(solution)/shard_map/ppermute | solution.py:710
  178.6 24.0 %layer_last.1 = (bf16[256,576]{1,0:T(8,128)(2,1)}, f32[2,576]{1,0:T(2,128)}, bf16[2,4,4,40,1536]{4,3,2,1,0:T(8,128)(2,1)}, bf16[2,4,4,40,1536]{4,3,2,1,0:T(8,128)(2,1)}) custom-call(s32[8]{0:T(128)} %stack.77.refs_0_, bf16[2,256,576]{2,1,0:T(8,128)(2,1)} %copy.36.refs_1_, f32[1,576]{1,0:T(1,128)} %refs_2_.11, f32[1,576]{1,0:T(1,128)} %refs_3_.11, ...), custom_call_target="tpu_custom_call" | custom-call | tf_op jit(solution)/shard_map/layer_last/pallas_call | solution.py:493
  209.7 3.4 %fusion.12 = (bf16[4,40,1536]{2,1,0:T(8,128)(2,1)S(1)}, bf16[4,40,1536]{2,1,0:T(8,128)(2,1)S(1)}, bf16[4,40,1536]{2,1,0:T(8,128)(2,1)S(1)}, bf16[4,40,1536]{2,1,0:T(8,128)(2,1)S(1)}) fusion(bf16[2,4,4,40,1536]{4,3,2,1,0:T(8,128)(2,1)S(1)} %collective-permute-done.12, bf16[2,4,4,40,1536]{4,3,2,1,0:T(8,128)(2,1)} %get-tuple-element.129), kind=kLoop, calls=%fused_computation.27 | loop fusion | flops 3932160 | bytes 5898240 | tf_op jit(solution)/shard_map/convert_element_type | solution.py:647
  213.7 2.0 collective-permute-start.21
  220.3 6.9 %collective-permute-done.18 = bf16[4,40,1536]{2,1,0:T(8,128)(2,1)S(1)} collective-permute-done((bf16[4,40,1536]{2,1,0:T(8,128)(2,1)S(1)}, bf16[4,40,1536]{2,1,0:T(8,128)(2,1)S(1)}, u32[]{:S(2)}, u32[]{:S(2)}) %collective-permute-start.18) | collective-permute-done | bytes 491552 | tf_op jit(solution)/shard_map/ppermute | solution.py:596
  227.2 2.1 fusion.2
  234.8 3.0 %collective-permute-done.16 = bf16[4,40,1536]{2,1,0:T(8,128)(2,1)S(1)} collective-permute-done((bf16[4,40,1536]{2,1,0:T(8,128)(2,1)S(1)}, bf16[4,40,1536]{2,1,0:T(8,128)(2,1)S(1)}, u32[]{:S(2)}, u32[]{:S(2)}) %collective-permute-start.16) | collective-permute-done | bytes 491552 | tf_op jit(solution)/shard_map/ppermute | solution.py:596
  238.3 2.9 %collective-permute-done.22 = bf16[4,40,1536]{2,1,0:T(8,128)(2,1)S(1)} collective-permute-done((bf16[4,40,1536]{2,1,0:T(8,128)(2,1)}, bf16[4,40,1536]{2,1,0:T(8,128)(2,1)S(1)}, u32[]{:S(2)}, u32[]{:S(2)}) %collective-permute-start.22) | collective-permute-done | bytes 491552 | tf_op jit(solution)/shard_map/ppermute | solution.py:596
  241.2 7.2 %collective-permute-done.24 = bf16[4,40,1536]{2,1,0:T(8,128)(2,1)} collective-permute-done((bf16[4,40,1536]{2,1,0:T(8,128)(2,1)S(1)}, bf16[4,40,1536]{2,1,0:T(8,128)(2,1)}, u32[]{:S(2)}, u32[]{:S(2)}) %collective-permute-start.24) | collective-permute-done | bytes 491552 | tf_op jit(solution)/shard_map/ppermute | solution.py:596
  248.4 3.0 %fusion.4 = (bf16[4,40,1536]{2,1,0:T(8,128)(2,1)}, bf16[4,40,1536]{2,1,0:T(8,128)(2,1)}) fusion(bf16[4,40,1536]{2,1,0:T(8,128)(2,1)S(1)} %collective-permute-done.22, bf16[4,40,1536]{2,1,0:T(8,128)(2,1)S(1)} %collective-permute-done.16, bf16[2,4,4,40,1536]{4,3,2,1,0:T(8,128)(2,1)} %copy-done, bf16[2,4,4,40,1536]{4,3,2,1,0:T(8,128)(2,1)} %get-tuple-element.129, ...), kind=kLoop, calls=%fused_computation.8 | loop fusion | flops 3440640 | bytes 4423680 | tf_op jit(solution)/shard_map/convert_element_type | solution.py:656
  251.4 1.9 collective-permute-start.23
  255.7 2.3 collective-permute-done.17
  258.0 16.7 %collective-permute-done.23 = bf16[4,40,1536]{2,1,0:T(8,128)(2,1)S(1)} collective-permute-done((bf16[4,40,1536]{2,1,0:T(8,128)(2,1)}, bf16[4,40,1536]{2,1,0:T(8,128)(2,1)S(1)}, u32[]{:S(2)}, u32[]{:S(2)}) %collective-permute-start.23) | collective-permute-done | bytes 491552 | tf_op jit(solution)/shard_map/ppermute | solution.py:596
  (131 shorter events, 60.0 us)
Async XLA Ops:
  7.2 73.8 %all-gather.3.cloned.1.call-start = ((), (), s32[]{:S(2)}) async-start(), calls=%async_computation | async-start | bytes 6266880 | tf_op jit(solution)/shard_map/all_gather | solution.py:608
  16.7 9.4 %collective-permute-start.5 = (bf16[96,576]{1,0:T(8,128)(2,1)S(1)}, bf16[96,576]{1,0:T(8,128)(2,1)S(1)}, u32[]{:S(2)}, u32[]{:S(2)}) collective-permute-start(bf16[96,576]{1,0:T(8,128)(2,1)S(1)} %reshape.154), channel_id=1, source_target_pairs={{0,12},{1,13},{2,14},{3,15},{4,8},{5,9},{6,10},{7,11},{8,4},{9,5},... | collective-permute-start | bytes 331784 | tf_op jit(solution)/shard_map/ppermute | solution.py:596
  21.8 15.5 %collective-permute-start.3 = (bf16[96,576]{1,0:T(8,128)(2,1)S(1)}, bf16[96,576]{1,0:T(8,128)(2,1)S(1)}, u32[]{:S(2)}, u32[]{:S(2)}) collective-permute-start(bf16[96,576]{1,0:T(8,128)(2,1)S(1)} %reshape.154), channel_id=1, source_target_pairs={{0,8},{1,9},{2,10},{3,11},{4,12},{5,13},{6,14},{7,15},{8,0},{9,1},... | collective-permute-start | bytes 331784 | tf_op jit(solution)/shard_map/ppermute | solution.py:596
  21.8 17.2 %collective-permute-start.1 = (bf16[96,576]{1,0:T(8,128)(2,1)S(1)}, bf16[96,576]{1,0:T(8,128)(2,1)S(1)}, u32[]{:S(2)}, u32[]{:S(2)}) collective-permute-start(bf16[96,576]{1,0:T(8,128)(2,1)S(1)} %reshape.154), channel_id=1, source_target_pairs={{0,4},{1,5},{2,6},{3,7},{4,0},{5,1},{6,2},{7,3},{8,12},{9,13},{10,... | collective-permute-start | bytes 331784 | tf_op jit(solution)/shard_map/ppermute | solution.py:596
  22.5 16.9 %collective-permute-start = (bf16[96,576]{1,0:T(8,128)(2,1)S(1)}, bf16[96,576]{1,0:T(8,128)(2,1)S(1)}, u32[]{:S(2)}, u32[]{:S(2)}) collective-permute-start(bf16[96,576]{1,0:T(8,128)(2,1)S(1)} %reshape.154), channel_id=1, source_target_pairs={{0,2},{1,3},{2,0},{3,1},{4,6},{5,7},{6,4},{7,5},{8,10},{9,11},{10,... | collective-permute-start | bytes 331784 | tf_op jit(solution)/shard_map/ppermute | solution.py:596
  26.1 18.0 %collective-permute-start.6 = (bf16[96,576]{1,0:T(8,128)(2,1)S(1)}, bf16[96,576]{1,0:T(8,128)(2,1)S(1)}, u32[]{:S(2)}, u32[]{:S(2)}) collective-permute-start(bf16[96,576]{1,0:T(8,128)(2,1)S(1)} %collective-permute-done.5), channel_id=1, source_target_pairs={{0,2},{1,3},{2,0},{3,1},{4,6},{5,7},{6,4},{7,5},{8,10},{9,11},{10,... | collective-permute-start | bytes 331784 | tf_op jit(solution)/shard_map/ppermute | solution.py:596
  37.3 6.7 %collective-permute-start.4 = (bf16[96,576]{1,0:T(8,128)(2,1)S(1)}, bf16[96,576]{1,0:T(8,128)(2,1)S(1)}, u32[]{:S(2)}, u32[]{:S(2)}) collective-permute-start(bf16[96,576]{1,0:T(8,128)(2,1)S(1)} %collective-permute-done.3), channel_id=1, source_target_pairs={{0,2},{1,3},{2,0},{3,1},{4,6},{5,7},{6,4},{7,5},{8,10},{9,11},{10,... | collective-permute-start | bytes 331784 | tf_op jit(solution)/shard_map/ppermute | solution.py:596
  39.1 4.9 %collective-permute-start.2 = (bf16[96,576]{1,0:T(8,128)(2,1)S(1)}, bf16[96,576]{1,0:T(8,128)(2,1)S(1)}, u32[]{:S(2)}, u32[]{:S(2)}) collective-permute-start(bf16[96,576]{1,0:T(8,128)(2,1)S(1)} %collective-permute-done.1), channel_id=1, source_target_pairs={{0,2},{1,3},{2,0},{3,1},{4,6},{5,7},{6,4},{7,5},{8,10},{9,11},{10,... | collective-permute-start | bytes 331784 | tf_op jit(solution)/shard_map/ppermute | solution.py:596
  44.1 5.2 %collective-permute-start.7 = (bf16[8,96,576]{2,1,0:T(8,128)(2,1)S(1)}, bf16[8,96,576]{2,1,0:T(8,128)(2,1)S(1)}, u32[]{:S(2)}, u32[]{:S(2)}) collective-permute-start(bf16[8,96,576]{2,1,0:T(8,128)(2,1)S(1)} %bitcast_dynamic-update-slice_fusion), channel_id=1, source_target_pairs={{0,1},{1,0},{2,3},{3,2},{4,5},{5,4},{6,7},{7,6},{8,9},{9,8},{10,11... | collective-permute-start | bytes 2654216 | tf_op jit(solution)/shard_map/ppermute | solution.py:596
  93.0 17.2 %collective-permute-start.9 = (bf16[256,576]{1,0:T(8,128)(2,1)}, bf16[256,576]{1,0:T(8,128)(2,1)S(1)}, u32[]{:S(2)}, u32[]{:S(2)}) collective-permute-start(bf16[256,576]{1,0:T(8,128)(2,1)} %get-tuple-element.98), channel_id=1, source_target_pairs={{0,16},{1,17},{2,18},{3,19},{4,20},{5,21},{6,22},{7,23},{8,24},{9,... | collective-permute-start | bytes 884744 | tf_op jit(solution)/shard_map/ppermute | solution.py:707
  107.4 27.5 %collective-permute-start.8 = (bf16[256,576]{1,0:T(8,128)(2,1)}, bf16[256,576]{1,0:T(8,128)(2,1)S(1)}, u32[]{:S(2)}, u32[]{:S(2)}) collective-permute-start(bf16[256,576]{1,0:T(8,128)(2,1)} %layer_lead.3), channel_id=1, source_target_pairs={{0,16},{1,17},{2,18},{3,19},{4,20},{5,21},{6,22},{7,23},{8,24},{9,... | collective-permute-start | bytes 884744 | tf_op jit(solution)/shard_map/ppermute | solution.py:707
  133.6 14.4 %collective-permute-start.10 = (bf16[256,576]{1,0:T(8,128)(2,1)}, bf16[256,576]{1,0:T(8,128)(2,1)S(1)}, u32[]{:S(2)}, u32[]{:S(2)}) collective-permute-start(bf16[256,576]{1,0:T(8,128)(2,1)} %get-tuple-element.101), channel_id=1, source_target_pairs={{16,0},{17,1},{18,2},{19,3},{20,4},{21,5},{22,6},{23,7},{24,8},{25... | collective-permute-start | bytes 884744 | tf_op jit(solution)/shard_map/ppermute | solution.py:710
  166.1 11.7 %collective-permute-start.11 = (bf16[256,576]{1,0:T(8,128)(2,1)}, bf16[256,576]{1,0:T(8,128)(2,1)S(1)}, u32[]{:S(2)}, u32[]{:S(2)}) collective-permute-start(bf16[256,576]{1,0:T(8,128)(2,1)} %get-tuple-element.108), channel_id=1, source_target_pairs={{16,0},{17,1},{18,2},{19,3},{20,4},{21,5},{22,6},{23,7},{24,8},{25... | collective-permute-start | bytes 884744 | tf_op jit(solution)/shard_map/ppermute | solution.py:710
  202.6 7.1 %collective-permute-start.12 = (bf16[2,4,4,40,1536]{4,3,2,1,0:T(8,128)(2,1)}, bf16[2,4,4,40,1536]{4,3,2,1,0:T(8,128)(2,1)S(1)}, u32[]{:S(2)}, u32[]{:S(2)}) collective-permute-start(bf16[2,4,4,40,1536]{4,3,2,1,0:T(8,128)(2,1)} %get-tuple-element.130), channel_id=1, source_target_pairs={{0,1},{1,0},{2,3},{3,2},{4,5},{5,4},{6,7},{7,6},{8,9},{9,8},{10,11... | collective-permute-start | bytes 11796488 | tf_op jit(solution)/shard_map/ppermute | solution.py:596
  205.5 4.0 %collective-permute-start.13 = (f32[2,576]{1,0:T(2,128)S(1)}, f32[2,576]{1,0:T(2,128)S(1)}, u32[]{:S(2)}, u32[]{:S(2)}) collective-permute-start(f32[2,576]{1,0:T(2,128)S(1)} %add.108), channel_id=1, source_target_pairs={{0,1},{1,0},{2,3},{3,2},{4,5},{5,4},{6,7},{7,6},{8,9},{9,8},{10,11... | collective-permute-start | bytes 13832 | tf_op jit(solution)/shard_map/ppermute | solution.py:596
  213.1 14.1 %collective-permute-start.18 = (bf16[4,40,1536]{2,1,0:T(8,128)(2,1)S(1)}, bf16[4,40,1536]{2,1,0:T(8,128)(2,1)S(1)}, u32[]{:S(2)}, u32[]{:S(2)}) collective-permute-start(bf16[4,40,1536]{2,1,0:T(8,128)(2,1)S(1)} %get-tuple-element.171), channel_id=1, source_target_pairs={{0,2},{1,3},{2,0},{3,1},{4,6},{5,7},{6,4},{7,5},{8,10},{9,11},{10,... | collective-permute-start | bytes 1474568 | tf_op jit(solution)/shard_map/ppermute | solution.py:596
  213.7 5.9 %collective-permute-start.21 = (f32[2,576]{1,0:T(2,128)S(1)}, f32[2,576]{1,0:T(2,128)S(1)}, u32[]{:S(2)}, u32[]{:S(2)}) collective-permute-start(f32[2,576]{1,0:T(2,128)S(1)} %add_add_fusion.1), channel_id=1, source_target_pairs={{0,12},{1,13},{2,14},{3,15},{4,8},{5,9},{6,10},{7,11},{8,4},{9,5},... | collective-permute-start | bytes 13832 | tf_op jit(solution)/shard_map/ppermute | solution.py:596
  215.7 4.5 %collective-permute-start.20 = (f32[2,576]{1,0:T(2,128)S(1)}, f32[2,576]{1,0:T(2,128)S(1)}, u32[]{:S(2)}, u32[]{:S(2)}) collective-permute-start(f32[2,576]{1,0:T(2,128)S(1)} %add_add_fusion.1), channel_id=1, source_target_pairs={{0,8},{1,9},{2,10},{3,11},{4,12},{5,13},{6,14},{7,15},{8,0},{9,1},... | collective-permute-start | bytes 13832 | tf_op jit(solution)/shard_map/ppermute | solution.py:596
  218.1 19.7 %collective-permute-start.16 = (bf16[4,40,1536]{2,1,0:T(8,128)(2,1)S(1)}, bf16[4,40,1536]{2,1,0:T(8,128)(2,1)S(1)}, u32[]{:S(2)}, u32[]{:S(2)}) collective-permute-start(bf16[4,40,1536]{2,1,0:T(8,128)(2,1)S(1)} %get-tuple-element.172), channel_id=1, source_target_pairs={{0,2},{1,3},{2,0},{3,1},{4,6},{5,7},{6,4},{7,5},{8,10},{9,11},{10,... | collective-permute-start | bytes 1474568 | tf_op jit(solution)/shard_map/ppermute | solution.py:596
  229.4 11.8 %collective-permute-start.22 = (bf16[4,40,1536]{2,1,0:T(8,128)(2,1)}, bf16[4,40,1536]{2,1,0:T(8,128)(2,1)S(1)}, u32[]{:S(2)}, u32[]{:S(2)}) collective-permute-start(bf16[4,40,1536]{2,1,0:T(8,128)(2,1)} %fusion.2), channel_id=1, source_target_pairs={{0,4},{1,5},{2,6},{3,7},{4,0},{5,1},{6,2},{7,3},{8,12},{9,13},{10,... | collective-permute-start | bytes 1474568 | tf_op jit(solution)/shard_map/ppermute | solution.py:596
  230.8 17.6 %collective-permute-start.24 = (bf16[4,40,1536]{2,1,0:T(8,128)(2,1)S(1)}, bf16[4,40,1536]{2,1,0:T(8,128)(2,1)}, u32[]{:S(2)}, u32[]{:S(2)}) collective-permute-start(bf16[4,40,1536]{2,1,0:T(8,128)(2,1)S(1)} %get-tuple-element.141), channel_id=1, source_target_pairs={{0,2},{1,3},{2,0},{3,1},{4,6},{5,7},{6,4},{7,5},{8,10},{9,11},{10,... | collective-permute-start | bytes 1474568 | tf_op jit(solution)/shard_map/ppermute | solution.py:596
  237.8 20.3 %collective-permute-start.17 = (bf16[4,40,1536]{2,1,0:T(8,128)(2,1)S(1)}, bf16[4,40,1536]{2,1,0:T(8,128)(2,1)S(1)}, u32[]{:S(2)}, u32[]{:S(2)}) collective-permute-start(bf16[4,40,1536]{2,1,0:T(8,128)(2,1)S(1)} %get-tuple-element.134), channel_id=1, source_target_pairs={{0,2},{1,3},{2,0},{3,1},{4,6},{5,7},{6,4},{7,5},{8,10},{9,11},{10,... | collective-permute-start | bytes 1474568 | tf_op jit(solution)/shard_map/ppermute | solution.py:596
  251.4 23.3 %collective-permute-start.23 = (bf16[4,40,1536]{2,1,0:T(8,128)(2,1)}, bf16[4,40,1536]{2,1,0:T(8,128)(2,1)S(1)}, u32[]{:S(2)}, u32[]{:S(2)}) collective-permute-start(bf16[4,40,1536]{2,1,0:T(8,128)(2,1)} %get-tuple-element.167), channel_id=1, source_target_pairs={{0,8},{1,9},{2,10},{3,11},{4,12},{5,13},{6,14},{7,15},{8,0},{9,1},... | collective-permute-start | bytes 1474568 | tf_op jit(solution)/shard_map/ppermute | solution.py:596
  253.3 21.4 %collective-permute-start.25 = (bf16[4,40,1536]{2,1,0:T(8,128)(2,1)}, bf16[4,40,1536]{2,1,0:T(8,128)(2,1)S(1)}, u32[]{:S(2)}, u32[]{:S(2)}) collective-permute-start(bf16[4,40,1536]{2,1,0:T(8,128)(2,1)} %get-tuple-element.168), channel_id=1, source_target_pairs={{0,4},{1,5},{2,6},{3,7},{4,0},{5,1},{6,2},{7,3},{8,12},{9,13},{10,... | collective-permute-start | bytes 1474568 | tf_op jit(solution)/shard_map/ppermute | solution.py:596
  (16 other events, 176.8 us)
Sparse Core Ops, SparseCore 0:
  16.0 64.8 all-gather.2

commit v2 on v1

--- a/solution.py
+++ b/solution.py
@@ -645,6 +645,7 @@
     gains = sum_of_four(gains, near)
     wide = [moved(gains, 1, 0, 0), moved(gains, 2, 0, 0), moved(gains, 3, 0, 0)]
     blocks = [add(keep[1, far], got[1, far]).astype(BF) for far in range(4)]
+    part_one = add(keep[0, 1], got[0, 1])
     across_three, across_two = moved(blocks[3], 0, 1, 0), moved(blocks[2], 0, 1, 0)
     across_three, wide = lax.optimization_barrier((across_three, wide))
     gains = sum_of_four(gains, wide)
@@ -653,8 +654,10 @@
     beside_three, across_one = moved(three, 1, 0, 0), moved(last_one, 0, 1, 0)
     across_two, last_zero = lax.optimization_barrier((across_two, blocks[0]))
     across_zero = moved(last_zero, 0, 1, 0)
-    far_two = moved(add(keep[0, 2], got[0, 2], across_two, beside_three).astype(BF), 2, 0, 0)
-    beside_one = moved(add(keep[0, 1], got[0, 1], across_one).astype(BF), 1, 0, 0)
+    two = add(keep[0, 2], got[0, 2], across_two, beside_three).astype(BF)
+    two, part_one = lax.optimization_barrier((two, part_one))
+    far_two = moved(two, 2, 0, 0)
+    beside_one = moved((part_one + across_one).astype(BF), 1, 0, 0)
     return add(keep[0, 0], got[0, 0], across_zero, far_two, beside_one), gains
 
 

time: 295 us -> 295 us (level)
    add x1 -> x2, other arithmetic: 1.47 us -> 6.07 us  [add(): return sum((term.astype(F32) for term in terms))]
    convert_element_type x2, other arithmetic: 6.43 us -> 2.3 us  [the longest x1 1.42 us: reduce_blocks(): two = add(keep[0, 2], got[0, 2], across_two, beside_three).astype(BF)]
    unnamed x39 -> x43, local copies, waits for them, and re-layouts: 7.09 us -> 7.12 us
  transfers between devices with their start and end apart: 27 -> 27, of which waited for: 17 -> 18; matrix products, arithmetic and copies ran while one was open for 6% -> 6% of each run, Pallas kernels for 16% -> 16%
where the time goes in v2:
time: 295 us; the launch traced here: 289 us
  Pallas kernels  98.3 us (33%)
  waiting for transfers between devices  78.7 us (27%)
  starting transfers between devices  32.9 us (11%)
  other arithmetic  25.8 us (9%)
  blocking collectives  23.2 us (8%)
  local copies, waits for them, and re-layouts  15.6 us (5%)
  between operations  15 us (5%)
    pallas_call x6, Pallas kernels, run_layer(): pl.pallas_call(kernel, out_shape=list(outs.values()), in_specs=[specs.get...  98.3 us
    ppermute x22, waiting for transfers between devices, moved(): lax.ppermute(value, 'dp', [(place_of(z, x, c), place_of(z ^ dz, x ^ dx, c...  59.8 us
    ppermute x22, starting transfers between devices, moved(): lax.ppermute(value, 'dp', [(place_of(z, x, c), place_of(z ^ dz, x ^ dx, c...  25.1 us
    all_gather x1, blocking collectives, gather_weights(): met = lax.all_gather(corner, 'dp', axis=0, tiled=False)  23.2 us
    ppermute x2, waiting for transfers between devices, send_back(): return lax.ppermute(block, 'section', [(1, 0)])  10.4 us
    all_gather x1, waiting for transfers between devices, gather_weights(): agu = lax.all_gather(packed, 'dp', axis=1, tiled=True)  8.44 us
    unnamed x7, other arithmetic  7.69 us
    unnamed x43, local copies, waits for them, and re-layouts  7.12 us
  transfers between devices with their start and end apart: 27, of which 18 were waited for; matrix products, arithmetic and copies ran while one was open for 6% of the time, Pallas kernels for 16%

profile of v2, /device:TPU:0, one launch (start us, length us, event | category | flops | bytes accessed | tf_op | source)
XLA Modules:
  0.0 289.4 jit_solution(4306209031906497364)
XLA Ops:
  16.7 5.1 %collective-permute-start.5 = (bf16[96,576]{1,0:T(8,128)(2,1)S(1)}, bf16[96,576]{1,0:T(8,128)(2,1)S(1)}, u32[]{:S(2)}, u32[]{:S(2)}) collective-permute-start(bf16[96,576]{1,0:T(8,128)(2,1)S(1)} %reshape.154), channel_id=1, source_target_pairs={{0,12},{1,13},{2,14},{3,15},{4,8},{5,9},{6,10},{7,11},{8,4},{9,5},... | collective-permute-start | bytes 331784 | tf_op jit(solution)/shard_map/ppermute | solution.py:596
  27.8 9.5 %collective-permute-done.3 = bf16[96,576]{1,0:T(8,128)(2,1)S(1)} collective-permute-done((bf16[96,576]{1,0:T(8,128)(2,1)S(1)}, bf16[96,576]{1,0:T(8,128)(2,1)S(1)}, u32[]{:S(2)}, u32[]{:S(2)}) %collective-permute-start.3) | collective-permute-done | bytes 110624 | tf_op jit(solution)/shard_map/ppermute | solution.py:596
  39.4 4.5 %collective-permute-done.2 = bf16[96,576]{1,0:T(8,128)(2,1)S(1)} collective-permute-done((bf16[96,576]{1,0:T(8,128)(2,1)S(1)}, bf16[96,576]{1,0:T(8,128)(2,1)S(1)}, u32[]{:S(2)}, u32[]{:S(2)}) %collective-permute-start.2) | collective-permute-done | bytes 110624 | tf_op jit(solution)/shard_map/ppermute | solution.py:596
  49.3 23.2 %all-gather = bf16[128,128]{1,0:T(8,128)(2,1)S(1)} all-gather(bf16[8,128]{1,0:T(8,128)(2,1)S(1)} %slice.138), channel_id=2, replica_groups=mesh['section'=2,'dp'=16] {'dp'}, dimensions={0}, use_global_device_ids=true | all-gather | bytes 34816 | tf_op jit(solution)/shard_map/all_gather | solution.py:614
  72.5 8.4 %all-gather.3.cloned.1.call-done.refs_4_ = bf16[3,640,1536]{2,1,0:T(8,128)(2,1)} async-done(((bf16[3,40,1536]{2,1,0:T(8,128)(2,1)}), bf16[3,640,1536]{2,1,0:T(8,128)(2,1)}) %all-gather.3.cloned.1.call-update) | async-done | bytes 5898256 | tf_op jit(solution)/shard_map/all_gather | solution.py:608
  82.1 11.0 %layer_lead.2 = (bf16[256,576]{1,0:T(8,128)(2,1)}, bf16[16,96,576]{2,1,0:T(8,128)(2,1)}) custom-call(s32[8]{0:T(128)} %stack.77.refs_0_, bf16[2,256,576]{2,1,0:T(8,128)(2,1)} %copy.36.refs_1_, f32[1,576]{1,0:T(1,128)} %refs_2_.11, f32[1,576]{1,0:T(1,128)} %refs_3_.11, bf16[3,640,1536]{2,1,0:T(8,128)(2,1)} %all-gather.3.cloned.1.call-done.refs_4_, ...), custom_call_target="tpu_custom_call" | custom-call | tf_op jit(solution)/shard_map/layer_lead/pallas_call | solution.py:493
  93.0 3.4 %collective-permute-start.9 = (bf16[256,576]{1,0:T(8,128)(2,1)}, bf16[256,576]{1,0:T(8,128)(2,1)S(1)}, u32[]{:S(2)}, u32[]{:S(2)}) collective-permute-start(bf16[256,576]{1,0:T(8,128)(2,1)} %get-tuple-element.100), channel_id=1, source_target_pairs={{0,16},{1,17},{2,18},{3,19},{4,20},{5,21},{6,22},{7,23},{8,24},{9,... | collective-permute-start | bytes 884744 | tf_op jit(solution)/shard_map/ppermute | solution.py:710
  96.5 10.9 %layer_lead.3 = bf16[256,576]{1,0:T(8,128)(2,1)} custom-call(s32[8]{0:T(128)} %stack.77.refs_0_, bf16[2,256,576]{2,1,0:T(8,128)(2,1)} %copy.36.refs_1_, f32[1,576]{1,0:T(1,128)} %refs_2_.11, f32[1,576]{1,0:T(1,128)} %refs_3_.11, bf16[3,640,1536]{2,1,0:T(8,128)(2,1)} %all-gather.3.cloned.1.call-done.refs_4_, bf16[16,96,576]{2,1,0:T(8,128)(2,1)} %get-tuple-element.98.refs_5_, ...), custom_call_target="tpu_custom_call" | custom-call | tf_op jit(solution)/shard_map/layer_lead/pallas_call | solution.py:493
  111.0 22.6 %layer_both.1 = (bf16[256,576]{1,0:T(8,128)(2,1)}, bf16[256,576]{1,0:T(8,128)(2,1)}, bf16[256,640]{1,0:T(8,128)(2,1)}, bf16[256,768]{1,0:T(8,128)(2,1)}, bf16[25...) custom-call(s32[8]{0:T(128)} %stack.77.refs_0_, ...), custom_call_target="tpu_custom_call" | custom-call | tf_op jit(solution)/shard_map/layer_both/pallas_call | solution.py:493
  135.7 12.3 %layer_ahead.1 = (bf16[256,576]{1,0:T(8,128)(2,1)}, bf16[256,640]{1,0:T(8,128)(2,1)}, bf16[256,768]{1,0:T(8,128)(2,1)}, bf16[256,192]{1,0:T(8,128)(2,1)}, f32[25...) custom-call(s32[8]{0:T(128)} %stack.77.refs_0_, ...), custom_call_target="tpu_custom_call" | custom-call | tf_op jit(solution)/shard_map/layer_ahead/pallas_call | solution.py:493
  148.8 17.4 %layer_behind.1 = (bf16[256,576]{1,0:T(8,128)(2,1)}, f32[2,576]{1,0:T(2,128)}, bf16[256,768]{1,0:T(8,128)(2,1)}, bf16[256,256]{1,0:T(8,128)(2,1)}, bf16[256,576]...) custom-call(s32[8]{0:T(128)} %stack.77.refs_0_, bf16[2,256,576]{2,1,0:T(8,128)(2,1)} %copy.36.refs_1_, ...), custom_call_target="tpu_custom_call" | custom-call | tf_op jit(solution)/shard_map/layer_behind/pallas_call | solution.py:493
  167.5 10.4 %collective-permute-done.11.refs_12_ = bf16[256,576]{1,0:T(8,128)(2,1)S(1)} collective-permute-done((bf16[256,576]{1,0:T(8,128)(2,1)}, bf16[256,576]{1,0:T(8,128)(2,1)S(1)}, u32[]{:S(2)}, u32[]{:S(2)}) %collective-permute-start.11) | collective-permute-done | bytes 294944 | tf_op jit(solution)/shard_map/ppermute | solution.py:713
  178.7 24.1 %layer_last.1 = (bf16[256,576]{1,0:T(8,128)(2,1)}, f32[2,576]{1,0:T(2,128)}, bf16[2,4,4,40,1536]{4,3,2,1,0:T(8,128)(2,1)}, bf16[2,4,4,40,1536]{4,3,2,1,0:T(8,128)(2,1)}) custom-call(s32[8]{0:T(128)} %stack.77.refs_0_, bf16[2,256,576]{2,1,0:T(8,128)(2,1)} %copy.36.refs_1_, f32[1,576]{1,0:T(1,128)} %refs_2_.11, f32[1,576]{1,0:T(1,128)} %refs_3_.11, ...), custom_call_target="tpu_custom_call" | custom-call | tf_op jit(solution)/shard_map/layer_last/pallas_call | solution.py:493
  207.8 1.8 collective-permute-done.13
  209.8 4.6 %add_bitcast_fusion = (f32[4,40,1536]{2,1,0:T(8,128)S(1)}, bf16[4,40,1536]{2,1,0:T(8,128)(2,1)}, bf16[4,40,1536]{2,1,0:T(8,128)(2,1)S(1)}, bf16[4,40,1536]{2,1,0:T(8,128)(2,1)}, bf16[4,40,1536]{2,1,0:T(8,128)(2,1)}) fusion(bf16[2,4,4,40,1536]{4,3,2,1,0:T(8,128)(2,1)S(1)} %collective-permute-done.12, bf16[2,4,4,40,1536]{4,3,2,1,0:T(8,128)(2,1)} %get-tuple-element.131), kind=kLoop, calls=%fused_computation.11 | loop fusion | flops 4669440 | bytes 7864320 | tf_op jit(solution)/shard_map/add | solution.py:634
  215.0 2.0 collective-permute-start.21
  221.6 6.9 %collective-permute-done.18 = bf16[4,40,1536]{2,1,0:T(8,128)(2,1)S(1)} collective-permute-done((bf16[4,40,1536]{2,1,0:T(8,128)(2,1)S(1)}, bf16[4,40,1536]{2,1,0:T(8,128)(2,1)S(1)}, u32[]{:S(2)}, u32[]{:S(2)}) %collective-permute-start.18) | collective-permute-done | bytes 491552 | tf_op jit(solution)/shard_map/ppermute | solution.py:596
  228.5 2.2 fusion.1
  235.1 3.9 %collective-permute-done.16 = bf16[4,40,1536]{2,1,0:T(8,128)(2,1)S(1)} collective-permute-done((bf16[4,40,1536]{2,1,0:T(8,128)(2,1)}, bf16[4,40,1536]{2,1,0:T(8,128)(2,1)S(1)}, u32[]{:S(2)}, u32[]{:S(2)}) %collective-permute-start.16) | collective-permute-done | bytes 491552 | tf_op jit(solution)/shard_map/ppermute | solution.py:596
  239.6 2.9 %collective-permute-done.22 = bf16[4,40,1536]{2,1,0:T(8,128)(2,1)S(1)} collective-permute-done((bf16[4,40,1536]{2,1,0:T(8,128)(2,1)}, bf16[4,40,1536]{2,1,0:T(8,128)(2,1)S(1)}, u32[]{:S(2)}, u32[]{:S(2)}) %collective-permute-start.22) | collective-permute-done | bytes 491552 | tf_op jit(solution)/shard_map/ppermute | solution.py:596
  244.0 5.6 %collective-permute-done.24 = bf16[4,40,1536]{2,1,0:T(8,128)(2,1)S(1)} collective-permute-done((bf16[4,40,1536]{2,1,0:T(8,128)(2,1)}, bf16[4,40,1536]{2,1,0:T(8,128)(2,1)S(1)}, u32[]{:S(2)}, u32[]{:S(2)}) %collective-permute-start.24) | collective-permute-done | bytes 491552 | tf_op jit(solution)/shard_map/ppermute | solution.py:596
  254.8 4.5 %collective-permute-done.17 = bf16[4,40,1536]{2,1,0:T(8,128)(2,1)S(1)} collective-permute-done((bf16[4,40,1536]{2,1,0:T(8,128)(2,1)}, bf16[4,40,1536]{2,1,0:T(8,128)(2,1)S(1)}, u32[]{:S(2)}, u32[]{:S(2)}) %collective-permute-start.17) | collective-permute-done | bytes 491552 | tf_op jit(solution)/shard_map/ppermute | solution.py:596
  259.3 13.0 %collective-permute-done.25 = bf16[4,40,1536]{2,1,0:T(8,128)(2,1)S(1)} collective-permute-done((bf16[4,40,1536]{2,1,0:T(8,128)(2,1)}, bf16[4,40,1536]{2,1,0:T(8,128)(2,1)S(1)}, u32[]{:S(2)}, u32[]{:S(2)}) %collective-permute-start.25) | collective-permute-done | bytes 491552 | tf_op jit(solution)/shard_map/ppermute | solution.py:596
  272.4 2.4 collective-permute-done.23
  (136 shorter events, 61.5 us)
Async XLA Ops:
  7.2 73.8 %all-gather.3.cloned.1.call-start = ((), (), s32[]{:S(2)}) async-start(), calls=%async_computation | async-start | bytes 6266880 | tf_op jit(solution)/shard_map/all_gather | solution.py:608
  16.7 9.4 %collective-permute-start.5 = (bf16[96,576]{1,0:T(8,128)(2,1)S(1)}, bf16[96,576]{1,0:T(8,128)(2,1)S(1)}, u32[]{:S(2)}, u32[]{:S(2)}) collective-permute-start(bf16[96,576]{1,0:T(8,128)(2,1)S(1)} %reshape.154), channel_id=1, source_target_pairs={{0,12},{1,13},{2,14},{3,15},{4,8},{5,9},{6,10},{7,11},{8,4},{9,5},... | collective-permute-start | bytes 331784 | tf_op jit(solution)/shard_map/ppermute | solution.py:596
  21.8 15.5 %collective-permute-start.3 = (bf16[96,576]{1,0:T(8,128)(2,1)S(1)}, bf16[96,576]{1,0:T(8,128)(2,1)S(1)}, u32[]{:S(2)}, u32[]{:S(2)}) collective-permute-start(bf16[96,576]{1,0:T(8,128)(2,1)S(1)} %reshape.154), channel_id=1, source_target_pairs={{0,8},{1,9},{2,10},{3,11},{4,12},{5,13},{6,14},{7,15},{8,0},{9,1},... | collective-permute-start | bytes 331784 | tf_op jit(solution)/shard_map/ppermute | solution.py:596
  21.8 17.2 %collective-permute-start.1 = (bf16[96,576]{1,0:T(8,128)(2,1)S(1)}, bf16[96,576]{1,0:T(8,128)(2,1)S(1)}, u32[]{:S(2)}, u32[]{:S(2)}) collective-permute-start(bf16[96,576]{1,0:T(8,128)(2,1)S(1)} %reshape.154), channel_id=1, source_target_pairs={{0,4},{1,5},{2,6},{3,7},{4,0},{5,1},{6,2},{7,3},{8,12},{9,13},{10,... | collective-permute-start | bytes 331784 | tf_op jit(solution)/shard_map/ppermute | solution.py:596
  22.5 16.9 %collective-permute-start = (bf16[96,576]{1,0:T(8,128)(2,1)S(1)}, bf16[96,576]{1,0:T(8,128)(2,1)S(1)}, u32[]{:S(2)}, u32[]{:S(2)}) collective-permute-start(bf16[96,576]{1,0:T(8,128)(2,1)S(1)} %reshape.154), channel_id=1, source_target_pairs={{0,2},{1,3},{2,0},{3,1},{4,6},{5,7},{6,4},{7,5},{8,10},{9,11},{10,... | collective-permute-start | bytes 331784 | tf_op jit(solution)/shard_map/ppermute | solution.py:596
  26.1 18.0 %collective-permute-start.6 = (bf16[96,576]{1,0:T(8,128)(2,1)S(1)}, bf16[96,576]{1,0:T(8,128)(2,1)S(1)}, u32[]{:S(2)}, u32[]{:S(2)}) collective-permute-start(bf16[96,576]{1,0:T(8,128)(2,1)S(1)} %collective-permute-done.5), channel_id=1, source_target_pairs={{0,2},{1,3},{2,0},{3,1},{4,6},{5,7},{6,4},{7,5},{8,10},{9,11},{10,... | collective-permute-start | bytes 331784 | tf_op jit(solution)/shard_map/ppermute | solution.py:596
  37.3 6.7 %collective-permute-start.4 = (bf16[96,576]{1,0:T(8,128)(2,1)S(1)}, bf16[96,576]{1,0:T(8,128)(2,1)S(1)}, u32[]{:S(2)}, u32[]{:S(2)}) collective-permute-start(bf16[96,576]{1,0:T(8,128)(2,1)S(1)} %collective-permute-done.3), channel_id=1, source_target_pairs={{0,2},{1,3},{2,0},{3,1},{4,6},{5,7},{6,4},{7,5},{8,10},{9,11},{10,... | collective-permute-start | bytes 331784 | tf_op jit(solution)/shard_map/ppermute | solution.py:596
  39.1 4.9 %collective-permute-start.2 = (bf16[96,576]{1,0:T(8,128)(2,1)S(1)}, bf16[96,576]{1,0:T(8,128)(2,1)S(1)}, u32[]{:S(2)}, u32[]{:S(2)}) collective-permute-start(bf16[96,576]{1,0:T(8,128)(2,1)S(1)} %collective-permute-done.1), channel_id=1, source_target_pairs={{0,2},{1,3},{2,0},{3,1},{4,6},{5,7},{6,4},{7,5},{8,10},{9,11},{10,... | collective-permute-start | bytes 331784 | tf_op jit(solution)/shard_map/ppermute | solution.py:596
  44.1 5.2 %collective-permute-start.7 = (bf16[8,96,576]{2,1,0:T(8,128)(2,1)S(1)}, bf16[8,96,576]{2,1,0:T(8,128)(2,1)S(1)}, u32[]{:S(2)}, u32[]{:S(2)}) collective-permute-start(bf16[8,96,576]{2,1,0:T(8,128)(2,1)S(1)} %bitcast_dynamic-update-slice_fusion), channel_id=1, source_target_pairs={{0,1},{1,0},{2,3},{3,2},{4,5},{5,4},{6,7},{7,6},{8,9},{9,8},{10,11... | collective-permute-start | bytes 2654216 | tf_op jit(solution)/shard_map/ppermute | solution.py:596
  93.0 17.2 %collective-permute-start.9 = (bf16[256,576]{1,0:T(8,128)(2,1)}, bf16[256,576]{1,0:T(8,128)(2,1)S(1)}, u32[]{:S(2)}, u32[]{:S(2)}) collective-permute-start(bf16[256,576]{1,0:T(8,128)(2,1)} %get-tuple-element.100), channel_id=1, source_target_pairs={{0,16},{1,17},{2,18},{3,19},{4,20},{5,21},{6,22},{7,23},{8,24},{9,... | collective-permute-start | bytes 884744 | tf_op jit(solution)/shard_map/ppermute | solution.py:710
  107.4 27.5 %collective-permute-start.8 = (bf16[256,576]{1,0:T(8,128)(2,1)}, bf16[256,576]{1,0:T(8,128)(2,1)S(1)}, u32[]{:S(2)}, u32[]{:S(2)}) collective-permute-start(bf16[256,576]{1,0:T(8,128)(2,1)} %layer_lead.3), channel_id=1, source_target_pairs={{0,16},{1,17},{2,18},{3,19},{4,20},{5,21},{6,22},{7,23},{8,24},{9,... | collective-permute-start | bytes 884744 | tf_op jit(solution)/shard_map/ppermute | solution.py:710
  133.6 14.4 %collective-permute-start.10 = (bf16[256,576]{1,0:T(8,128)(2,1)}, bf16[256,576]{1,0:T(8,128)(2,1)S(1)}, u32[]{:S(2)}, u32[]{:S(2)}) collective-permute-start(bf16[256,576]{1,0:T(8,128)(2,1)} %get-tuple-element.103), channel_id=1, source_target_pairs={{16,0},{17,1},{18,2},{19,3},{20,4},{21,5},{22,6},{23,7},{24,8},{25... | collective-permute-start | bytes 884744 | tf_op jit(solution)/shard_map/ppermute | solution.py:713
  166.2 11.7 %collective-permute-start.11 = (bf16[256,576]{1,0:T(8,128)(2,1)}, bf16[256,576]{1,0:T(8,128)(2,1)S(1)}, u32[]{:S(2)}, u32[]{:S(2)}) collective-permute-start(bf16[256,576]{1,0:T(8,128)(2,1)} %get-tuple-element.110), channel_id=1, source_target_pairs={{16,0},{17,1},{18,2},{19,3},{20,4},{21,5},{22,6},{23,7},{24,8},{25... | collective-permute-start | bytes 884744 | tf_op jit(solution)/shard_map/ppermute | solution.py:713
  202.7 7.1 %collective-permute-start.12 = (bf16[2,4,4,40,1536]{4,3,2,1,0:T(8,128)(2,1)}, bf16[2,4,4,40,1536]{4,3,2,1,0:T(8,128)(2,1)S(1)}, u32[]{:S(2)}, u32[]{:S(2)}) collective-permute-start(bf16[2,4,4,40,1536]{4,3,2,1,0:T(8,128)(2,1)} %get-tuple-element.132), channel_id=1, source_target_pairs={{0,1},{1,0},{2,3},{3,2},{4,5},{5,4},{6,7},{7,6},{8,9},{9,8},{10,11... | collective-permute-start | bytes 11796488 | tf_op jit(solution)/shard_map/ppermute | solution.py:596
  205.6 4.0 %collective-permute-start.13 = (f32[2,576]{1,0:T(2,128)S(1)}, f32[2,576]{1,0:T(2,128)S(1)}, u32[]{:S(2)}, u32[]{:S(2)}) collective-permute-start(f32[2,576]{1,0:T(2,128)S(1)} %add.108), channel_id=1, source_target_pairs={{0,1},{1,0},{2,3},{3,2},{4,5},{5,4},{6,7},{7,6},{8,9},{9,8},{10,11... | collective-permute-start | bytes 13832 | tf_op jit(solution)/shard_map/ppermute | solution.py:596
  214.4 14.1 %collective-permute-start.18 = (bf16[4,40,1536]{2,1,0:T(8,128)(2,1)S(1)}, bf16[4,40,1536]{2,1,0:T(8,128)(2,1)S(1)}, u32[]{:S(2)}, u32[]{:S(2)}) collective-permute-start(bf16[4,40,1536]{2,1,0:T(8,128)(2,1)S(1)} %get-tuple-element.173), channel_id=1, source_target_pairs={{0,2},{1,3},{2,0},{3,1},{4,6},{5,7},{6,4},{7,5},{8,10},{9,11},{10,... | collective-permute-start | bytes 1474568 | tf_op jit(solution)/shard_map/ppermute | solution.py:596
  215.0 5.9 %collective-permute-start.21 = (f32[2,576]{1,0:T(2,128)S(1)}, f32[2,576]{1,0:T(2,128)S(1)}, u32[]{:S(2)}, u32[]{:S(2)}) collective-permute-start(f32[2,576]{1,0:T(2,128)S(1)} %add_add_fusion.1), channel_id=1, source_target_pairs={{0,12},{1,13},{2,14},{3,15},{4,8},{5,9},{6,10},{7,11},{8,4},{9,5},... | collective-permute-start | bytes 13832 | tf_op jit(solution)/shard_map/ppermute | solution.py:596
  217.0 4.5 %collective-permute-start.20 = (f32[2,576]{1,0:T(2,128)S(1)}, f32[2,576]{1,0:T(2,128)S(1)}, u32[]{:S(2)}, u32[]{:S(2)}) collective-permute-start(f32[2,576]{1,0:T(2,128)S(1)} %add_add_fusion.1), channel_id=1, source_target_pairs={{0,8},{1,9},{2,10},{3,11},{4,12},{5,13},{6,14},{7,15},{8,0},{9,1},... | collective-permute-start | bytes 13832 | tf_op jit(solution)/shard_map/ppermute | solution.py:596
  219.4 19.6 %collective-permute-start.16 = (bf16[4,40,1536]{2,1,0:T(8,128)(2,1)}, bf16[4,40,1536]{2,1,0:T(8,128)(2,1)S(1)}, u32[]{:S(2)}, u32[]{:S(2)}) collective-permute-start(bf16[4,40,1536]{2,1,0:T(8,128)(2,1)} %get-tuple-element.175), channel_id=1, source_target_pairs={{0,2},{1,3},{2,0},{3,1},{4,6},{5,7},{6,4},{7,5},{8,10},{9,11},{10,... | collective-permute-start | bytes 1474568 | tf_op jit(solution)/shard_map/ppermute | solution.py:596
  230.7 11.8 %collective-permute-start.22 = (bf16[4,40,1536]{2,1,0:T(8,128)(2,1)}, bf16[4,40,1536]{2,1,0:T(8,128)(2,1)S(1)}, u32[]{:S(2)}, u32[]{:S(2)}) collective-permute-start(bf16[4,40,1536]{2,1,0:T(8,128)(2,1)} %fusion.1), channel_id=1, source_target_pairs={{0,4},{1,5},{2,6},{3,7},{4,0},{5,1},{6,2},{7,3},{8,12},{9,13},{10,... | collective-permute-start | bytes 1474568 | tf_op jit(solution)/shard_map/ppermute | solution.py:596
  234.5 15.1 %collective-permute-start.24 = (bf16[4,40,1536]{2,1,0:T(8,128)(2,1)}, bf16[4,40,1536]{2,1,0:T(8,128)(2,1)S(1)}, u32[]{:S(2)}, u32[]{:S(2)}) collective-permute-start(bf16[4,40,1536]{2,1,0:T(8,128)(2,1)} %get-tuple-element.145), channel_id=1, source_target_pairs={{0,2},{1,3},{2,0},{3,1},{4,6},{5,7},{6,4},{7,5},{8,10},{9,11},{10,... | collective-permute-start | bytes 1474568 | tf_op jit(solution)/shard_map/ppermute | solution.py:596
  239.1 20.3 %collective-permute-start.17 = (bf16[4,40,1536]{2,1,0:T(8,128)(2,1)}, bf16[4,40,1536]{2,1,0:T(8,128)(2,1)S(1)}, u32[]{:S(2)}, u32[]{:S(2)}) collective-permute-start(bf16[4,40,1536]{2,1,0:T(8,128)(2,1)} %get-tuple-element.136), channel_id=1, source_target_pairs={{0,2},{1,3},{2,0},{3,1},{4,6},{5,7},{6,4},{7,5},{8,10},{9,11},{10,... | collective-permute-start | bytes 1474568 | tf_op jit(solution)/shard_map/ppermute | solution.py:596
  250.5 21.9 %collective-permute-start.25 = (bf16[4,40,1536]{2,1,0:T(8,128)(2,1)}, bf16[4,40,1536]{2,1,0:T(8,128)(2,1)S(1)}, u32[]{:S(2)}, u32[]{:S(2)}) collective-permute-start(bf16[4,40,1536]{2,1,0:T(8,128)(2,1)} %add_convert_fusion), channel_id=1, source_target_pairs={{0,4},{1,5},{2,6},{3,7},{4,0},{5,1},{6,2},{7,3},{8,12},{9,13},{10,... | collective-permute-start | bytes 1474568 | tf_op jit(solution)/shard_map/ppermute | solution.py:596
  251.9 22.8 %collective-permute-start.23 = (bf16[4,40,1536]{2,1,0:T(8,128)(2,1)S(1)}, bf16[4,40,1536]{2,1,0:T(8,128)(2,1)S(1)}, u32[]{:S(2)}, u32[]{:S(2)}) collective-permute-start(bf16[4,40,1536]{2,1,0:T(8,128)(2,1)S(1)} %fusion.3), channel_id=1, source_target_pairs={{0,8},{1,9},{2,10},{3,11},{4,12},{5,13},{6,14},{7,15},{8,0},{9,1},... | collective-permute-start | bytes 1474568 | tf_op jit(solution)/shard_map/ppermute | solution.py:596
  (18 other events, 198.0 us)
Sparse Core Ops, SparseCore 0:
  16.0 64.8 all-gather.2
